TPU v7x, 256 devices: a whole 4x4x8 slice. The times are simulated.
256 devices in a mesh: dp: 8 (over y, core), expert: 32 (over x, z).
Axes of the slice: x: 4, y: 4, z: 8, core: 2. Of those that a mesh axis runs over, the one named last changes fastest.
Arguments:
- inputs: bfloat16 [512, 2304], P('dp'), may hold values from -90 to 90
- tail_inputs: bfloat16 [256, 2304], P('dp'), may hold values from -90 to 90
- states: bfloat16 [512, 32, 128, 128], P('dp', 'expert'), may hold values from -18 to 18
- tail_ids: int32 [256], replicated, may hold values from 0 to 511, as said below
- routes: int32 [512, 8], replicated, may hold values from 0 to 127, all different within a row; in each aligned block of 64 rows (0 to 63, 64 to 127, ...) at most 8 rows name the same one
- tail_routes: int32 [256, 8], replicated, may hold values from 0 to 127, all different within a row; in each aligned block of 32 rows (0 to 31, 32 to 63, ...) at most 4 rows name the same one
- attention_gain: float32 [2304], replicated, may hold values from 0.1 to 1.9
- query_weight: bfloat16 [2304, 4096], P(None, 'expert'), may hold values from -0.125 to 0.125
- key_weight: bfloat16 [2304, 4096], P(None, 'expert'), may hold values from -0.125 to 0.125
- value_weight: bfloat16 [2304, 4096], P(None, 'expert'), may hold values from -0.125 to 0.125
- decay_down: bfloat16 [2304, 128], replicated, may hold values from -0.125 to 0.125
- decay_up: bfloat16 [128, 4096], P(None, 'expert'), may hold values from -0.5 to 0.5
- decay_bias: float32 [4096], P('expert'), may hold values from -4 to 4
- decay_log: float32 [32], P('expert'), may hold values from -3 to 0.5
- beta_weight: bfloat16 [2304, 32], P(None, 'expert'), may hold values from -0.125 to 0.125
- output_gain: float32 [128], replicated, may hold values from 0.1 to 1.9
- head_out: bfloat16 [4096, 2304], P('expert'), may hold values from -0.09375 to 0.09375
- expert_gain: float32 [2304], replicated, may hold values from 0.1 to 1.9
- router_weight: bfloat16 [2304, 128], replicated, may hold values from -0.125 to 0.125
- gate_weight: bfloat16 [128, 2304, 1024], P('expert', None, 'dp'), may hold values from -0.125 to 0.125
- up_weight: bfloat16 [128, 2304, 1024], P('expert', None, 'dp'), may hold values from -0.125 to 0.125
- down_weight: bfloat16 [128, 1024, 2304], P('expert', 'dp'), may hold values from -0.1875 to 0.1875
Outputs:
- first_out: bfloat16 [512, 2304], P(('dp', 'expert'))
- tail_out: bfloat16 [256, 2304], P(('dp', 'expert'))
Inputs may be any that keep to these rules, and one draw needn't show every extreme that they name: `tail_ids`: distinct row ids. Position p belongs to destination group p // 32; a destination's 32 positions form 4 aligned runs of 8, each run from one source group (id // 64), the four sources distinct, so at most 8 tail rows go from one group to another and that count is reached. `routes`: in each aligned block of 64 rows (one group's rows) no expert is named by more than 8 rows, and that count is reached. `tail_routes`: in each aligned block of 32 rows no expert is named by more than 4 rows, and that count is reached.
All inputs are finite; a program needn't handle non-finite values.
Results may differ from a plain program's by a relative error of at most 0.015.
Values may be sent and summed in bfloat16 or wider, within the bound.
A program may use at most 128 MiB of HBM per device.

v0:
```python
import jax
import jax.numpy as jnp
from jax import lax
from jax.sharding import PartitionSpec as P

epsilon = 1e-06
route_scale = 2.446
exact_mode = lax.Precision.HIGHEST


def rms_rows(source, gain):
    wide = source.astype(jnp.float32)
    factor = lax.rsqrt(jnp.mean(wide * wide, axis=-1, keepdims=True) + epsilon)
    return (wide * factor * gain).astype(jnp.bfloat16)


def unit_rows(source):
    return source * lax.rsqrt(jnp.sum(source * source, axis=-1, keepdims=True) + epsilon)


def delta_step(normed, state_rows, layer):
    (
        attention_gain,
        query_weight,
        key_weight,
        value_weight,
        decay_down,
        decay_up,
        decay_bias,
        decay_log,
        beta_weight,
        output_gain,
        head_out,
    ) = layer
    row_count = normed.shape[0]
    head_count = state_rows.shape[1]
    head_width = state_rows.shape[2]

    def project(weight):
        produced = jnp.dot(normed, weight, preferred_element_type=jnp.float32)
        return jax.nn.silu(produced).reshape(row_count, head_count, head_width)

    query_rows = unit_rows(project(query_weight))
    key_rows = unit_rows(project(key_weight))
    value_rows = project(value_weight)
    lowrank = jnp.dot(normed, decay_down, preferred_element_type=jnp.float32).astype(jnp.bfloat16)
    gate_input = jnp.dot(lowrank, decay_up, preferred_element_type=jnp.float32) + decay_bias
    decay_rate = jnp.exp(decay_log)[None, :, None] * jax.nn.softplus(
        gate_input.reshape(row_count, head_count, head_width)
    )
    decay_rows = jnp.exp(-decay_rate)
    beta_rows = jax.nn.sigmoid(jnp.dot(normed, beta_weight, preferred_element_type=jnp.float32))
    kept_state = decay_rows[..., None] * state_rows.astype(jnp.float32)
    recalled = jnp.einsum("rhkv,rhk->rhv", kept_state, key_rows, precision=exact_mode)
    update = (beta_rows[..., None] * key_rows)[..., None] * (value_rows - recalled)[..., None, :]
    fresh_state = kept_state + update
    readout = jnp.einsum(
        "rhkv,rhk->rhv", fresh_state, query_rows, precision=exact_mode
    ) * head_width ** (-0.5)
    normed_out = readout * lax.rsqrt(jnp.mean(readout * readout, axis=-1, keepdims=True) + epsilon)
    normed_out = normed_out * output_gain
    return (
        normed_out.astype(jnp.bfloat16).reshape(row_count, head_count * head_width),
        fresh_state,
    )


def attend(tokens, state_rows, layer):
    normed = rms_rows(tokens, layer[0])
    head_rows, fresh_state = delta_step(normed, state_rows, layer)
    partial_value = jnp.dot(head_rows, layer[10], preferred_element_type=jnp.float32)
    summed = lax.psum(partial_value.astype(jnp.bfloat16), "expert").astype(jnp.float32)
    hidden = (tokens.astype(jnp.float32) + summed).astype(jnp.bfloat16)
    return (hidden, fresh_state.astype(jnp.bfloat16))


def slot_tables(route_table, group_rows, capacity, expert_ids):
    group_count = route_table.shape[0] // group_rows
    blocked = route_table.reshape(group_count, group_rows, route_table.shape[1])
    named_rows = jnp.any(blocked[:, :, :, None] == expert_ids[None, None, None, :], axis=2)
    named_rows = jnp.transpose(named_rows, (0, 2, 1))
    ranked = jnp.cumsum(named_rows.astype(jnp.int32), axis=2) - 1
    places = jnp.arange(capacity, dtype=jnp.int32)
    select = named_rows[:, :, None, :] & (ranked[:, :, None, :] == places[None, None, :, None])
    positions = jnp.arange(group_rows, dtype=jnp.int32)
    token_index = jnp.sum(jnp.where(select, positions, 0), axis=3)
    filled = jnp.any(select, axis=3)
    group_index = jnp.arange(group_count, dtype=jnp.int32)[:, None, None]
    slot_routes = blocked[group_index, token_index]
    return (select, filled, slot_routes)


def slot_weights(slot_values, slot_routes, expert_ids, router_weight):
    logits = jnp.einsum(
        "gecd,dn->gecn", slot_values, router_weight, preferred_element_type=jnp.float32
    )
    scores = jax.nn.sigmoid(logits)
    chosen = jnp.take_along_axis(scores, slot_routes, axis=-1)
    shares = route_scale * chosen / jnp.sum(chosen, axis=-1, keepdims=True)
    return jnp.sum(jnp.where(slot_routes == expert_ids[None, :, None, None], shares, 0.0), axis=-1)


def expert_apply(slot_values, weights, gate_weight, up_weight, down_weight):
    gate_rows = jnp.einsum(
        "gecd,edf->gecf", slot_values, gate_weight, preferred_element_type=jnp.float32
    )
    up_rows = jnp.einsum(
        "gecd,edf->gecf", slot_values, up_weight, preferred_element_type=jnp.float32
    )
    active = (jax.nn.silu(gate_rows) * up_rows).astype(jnp.bfloat16)
    produced = jnp.einsum("gecf,efd->gecd", active, down_weight, preferred_element_type=jnp.float32)
    return produced * weights[..., None]


def mixture(blocks, experts):
    expert_gain, router_weight, gate_weight, up_weight, down_weight = experts
    own_group = lax.axis_index("dp")
    column_count = lax.axis_size("expert")
    column_index = lax.axis_index("expert")
    local_experts = gate_weight.shape[0]
    feature_count = gate_weight.shape[1]
    expert_ids = column_index * local_experts + jnp.arange(local_experts, dtype=jnp.int32)
    prepared = []
    outgoing = []
    for hidden, route_table in blocks:
        group_rows = hidden.shape[0]
        capacity = 2 * group_rows * route_table.shape[1] // router_weight.shape[1]
        select, filled, slot_routes = slot_tables(route_table, group_rows, capacity, expert_ids)
        normed = rms_rows(hidden, expert_gain)
        own_select = lax.dynamic_index_in_dim(select, own_group, 0, keepdims=False)
        picked = jnp.einsum(
            "ecr,rd->ecd",
            own_select.astype(jnp.bfloat16),
            normed,
            preferred_element_type=jnp.float32,
        )
        outgoing.append(
            picked.astype(jnp.bfloat16).reshape(local_experts * capacity, feature_count)
        )
        prepared.append((hidden, select, filled, slot_routes, capacity))
    sent_rows = outgoing[0]
    per_group = sent_rows.shape[0]
    gathered = lax.all_gather(sent_rows, "dp", axis=0, tiled=True)
    segment = gathered
    segment = segment.reshape(
        per_group * lax.axis_size("dp") // per_group, per_group, feature_count
    )
    hidden, select, filled, slot_routes, capacity = prepared[0]
    block_width = local_experts * capacity
    slot_values = segment.reshape(
        per_group * lax.axis_size("dp") // per_group, local_experts, capacity, feature_count
    )
    routes_here = slot_routes
    filled_here = filled
    weights = jnp.where(
        filled_here, slot_weights(slot_values, routes_here, expert_ids, router_weight), 0.0
    )
    produced = expert_apply(slot_values, weights, gate_weight, up_weight, down_weight)
    results = produced.reshape(
        per_group * lax.axis_size("dp") // per_group, block_width, feature_count
    )
    own_sums = lax.psum_scatter(
        results.reshape(per_group * lax.axis_size("dp"), feature_count).astype(jnp.bfloat16),
        "dp",
        scatter_dimension=0,
        tiled=True,
    ).astype(jnp.float32)
    hidden, select, filled, slot_routes, capacity = prepared[0]
    own_select = lax.dynamic_index_in_dim(select, own_group, 0, keepdims=False).astype(jnp.float32)
    own_out = own_sums.reshape(local_experts, capacity, feature_count)
    token_sums = jnp.einsum("ecr,ecd->rd", own_select, own_out, precision=exact_mode)
    token_parts = token_sums.reshape(column_count, -1, feature_count)
    share_sums = lax.psum_scatter(
        token_parts.reshape(-1, feature_count).astype(jnp.bfloat16),
        "expert",
        scatter_dimension=0,
        tiled=True,
    ).astype(jnp.float32)
    hidden, select, filled, slot_routes, capacity = prepared[0]
    share_rows = hidden.shape[0] // column_count
    own_hidden = lax.dynamic_slice_in_dim(hidden, column_index * share_rows, share_rows, 0)
    summed = own_hidden.astype(jnp.float32) + share_sums
    finals = [summed.astype(jnp.bfloat16)]
    return finals


def source_rows(updated, tail_ids, tail_rows):
    group_count = lax.axis_size("dp")
    own_group = lax.axis_index("dp")
    group_rows = updated.shape[0]
    run_length = tail_rows // 4
    run_table = tail_ids.reshape(group_count, 4, run_length)
    sources = run_table[:, :, 0] // group_rows
    matched = sources == own_group
    local_rows = jnp.sum(
        jnp.where(matched[:, :, None], run_table - own_group * group_rows, 0), axis=1
    )
    filled = jnp.any(matched, axis=1)
    picked = jnp.take(updated, jnp.clip(local_rows, 0, group_rows - 1).reshape(-1), axis=0)
    return (picked, jnp.repeat(filled, run_length))


def list_places(tail_ids, group_rows, tail_rows):
    own_group = lax.axis_index("dp")
    run_length = tail_rows // 4
    own_ids = lax.dynamic_slice_in_dim(tail_ids, own_group * tail_rows, tail_rows, 0)
    anchor = own_ids // group_rows
    return anchor * run_length + jnp.arange(tail_rows, dtype=jnp.int32) % run_length


def migrate(updated, tail_ids, tail_rows):
    picked, keep_rows = source_rows(updated, tail_ids, tail_rows)
    picked = jnp.where(keep_rows[:, None, None, None], picked, jnp.zeros_like(picked))
    arrived = lax.all_to_all(picked, "dp", split_axis=0, concat_axis=0, tiled=True)
    return jnp.take(arrived, list_places(tail_ids, updated.shape[0], tail_rows), axis=0)


def on_device(
    inputs,
    tail_inputs,
    states,
    tail_ids,
    routes,
    tail_routes,
    attention_gain,
    query_weight,
    key_weight,
    value_weight,
    decay_down,
    decay_up,
    decay_bias,
    decay_log,
    beta_weight,
    output_gain,
    head_out,
    expert_gain,
    router_weight,
    gate_weight,
    up_weight,
    down_weight,
):
    layer = (
        attention_gain,
        query_weight,
        key_weight,
        value_weight,
        decay_down,
        decay_up,
        decay_bias,
        decay_log,
        beta_weight,
        output_gain,
        head_out,
    )
    experts = (expert_gain, router_weight, gate_weight, up_weight, down_weight)
    first_hidden, updated = attend(inputs, states, layer)
    first_out = mixture(((first_hidden, routes),), experts)[0]
    tail_state = migrate(updated, tail_ids, tail_inputs.shape[0])
    tail_hidden, unused = attend(tail_inputs, tail_state, layer)
    tail_out = mixture(((tail_hidden, tail_routes),), experts)[0]
    return (first_out, tail_out)


def solution(mesh):
    placed = (
        P("dp", None),
        P("dp", None),
        P("dp", "expert", None, None),
        P(),
        P(),
        P(),
        P(),
        P(None, "expert"),
        P(None, "expert"),
        P(None, "expert"),
        P(),
        P(None, "expert"),
        P("expert"),
        P("expert"),
        P(None, "expert"),
        P(),
        P("expert", None),
        P(),
        P(),
        P("expert", None, "dp"),
        P("expert", None, "dp"),
        P("expert", "dp", None),
    )
    return jax.shard_map(
        on_device,
        mesh=mesh,
        in_specs=placed,
        out_specs=(P(("dp", "expert"), None), P(("dp", "expert"), None)),
        check_vma=False,
    )
```

profile of v0, /device:TPU:1, one launch (start us, length us, event | category | flops | bytes accessed | tf_op | source)
XLA Modules:
  0.0 485.1 jit_solution(15794601732919710044)
XLA Ops:
  15.3 5.8 %fusion.4 = f32[64,1,128]{2,1,0:T(1,128)S(1)} fusion(f32[64,128,1]{1,2,0:T(1,128)S(1)} %bitcast.253, bf16[64,1,128,128]{3,2,1,0:T(8,128)(2,1)} %param.24, f32[64,128]{1,0:T(8,128)S(1)} %fusion.127), kind=kOutput, calls=%fused_computation.10 | convolution fusion | flops 14680064 | bytes 2195456 | tf_op jit(solution)/shard_map/rhkv,rhk->rhv/dot_general | solution.py:54
  22.4 3.5 fusion.24
  25.9 3.7 gather_fusion.1
  29.6 3.2 fusion.25
  32.8 7.6 %all-to-all-start = ((bf16[64,1,128,128]{3,2,1,0:T(8,128)(2,1)}), bf16[64,1,128,128]{3,2,1,0:T(8,128)(2,1)}, u32[]{:S(2)}, u32[]{:S(2)}) async-start(bf16[64,1,128,128]{3,2,1,0:T(8,128)(2,1)} %fusion.25), calls=%async_computation.1 | async-start | bytes 4194304 | tf_op jit(solution)/shard_map/all_to_all | solution.py:214
  40.6 2.1 multiply_reduce_fusion.5
  42.7 2.6 multiply_reduce_fusion.4
  47.5 6.5 %fusion.2 = f32[64,1,128]{2,1,0:T(1,128)S(1)} fusion(f32[64,128,1]{1,2,0:T(1,128)S(1)} %bitcast.254, bf16[64,1,128,128]{3,2,1,0:T(8,128)(2,1)} %param.24, f32[64,128]{1,0:T(8,128)S(1)} %multiply_subtract_fusion, f32[64,128]{1,0:T(8,128)S(1)} %get-tuple-element.16, f32[64,128]{1,0:T(8,128)S(1)} %fusion.127), kind=kOutput, calls=%fused_computation.8 | convolution fusion | flops 16777216 | bytes 2260992 | tf_op jit(solution)/shard_map/rhkv,rhk->rhv/dot_general | solution.py:57
  61.3 1.9 gather_fusion
  70.3 3.3 gather_fusion.2
  73.5 3.5 fusion.29
  77.4 2.9 fusion.26
  83.7 141.6 %all-reduce.9.cloned.1.call-done = (bf16[64,2304]{1,0:T(8,128)(2,1)}, bf16[32,2304]{1,0:T(8,128)(2,1)}) async-done(((bf16[64,2304]{1,0:T(8,128)(2,1)}, bf16[32,2304]{1,0:T(8,128)(2,1)}), (bf16[64,2304]{1,0:T(8,128)(2,1)}, bf16[32,2304]{1,0:T(8,128)(2,1)})) %all-reduce.9.cloned.1.call-update) | async-done | bytes 442384 | tf_op jit(solution)/shard_map/psum | solution.py:72
  229.7 18.7 %all_gather.7 = bf16[128,2304]{1,0:T(8,128)(2,1)S(1)} all-gather(bf16[16,2304]{1,0:T(8,128)(2,1)S(1)} %reshape.437), channel_id=1, replica_groups=mesh['dp'=8,'expert'=32] {'dp'}, dimensions={0}, use_global_device_ids=true | all-gather | bytes 663552 | tf_op jit(solution)/shard_map/all_gather | solution.py:143
  250.0 8.0 %gather_fusion.5 = f32[1024]{0:T(1024)S(1)} fusion(f32[8,4,4,128]{3,0,2,1:T(8,128)S(1)} %fusion.117, s32[1024]{0:T(1024)S(1)} %reshape.477), kind=kCustom, calls=%fused_computation.5 | custom fusion | bytes 24576 | tf_op jit(solution)/shard_map/jit(take_along_axis)/gather | solution.py:98
  258.6 2.4 fusion.16
  265.1 15.7 %gather_fusion.4 = f32[2048]{0:T(1024)S(1)} fusion(f32[8,4,8,128]{3,2,0,1:T(8,128)S(1)} %fusion.47, s32[2048]{0:T(1024)S(1)} %reshape.471), kind=kCustom, calls=%fused_computation.4 | custom fusion | bytes 49152 | tf_op jit(solution)/shard_map/jit(take_along_axis)/gather | solution.py:98
  281.3 3.3 fusion.36
  284.5 3.6 fusion.8
  288.1 2.4 copy.168
  294.0 33.4 %reduce-scatter.3.cloned.1.call-done = bf16[32,2304]{1,0:T(8,128)(2,1)} async-done(((bf16[256,2304]{1,0:T(8,128)(2,1)}), bf16[32,2304]{1,0:T(8,128)(2,1)}) %reduce-scatter.3.cloned.1.call-update) | async-done | bytes 147472 | tf_op jit(solution)/shard_map/reduce_scatter | solution.py:162
  327.4 1.9 fusion.11
  330.6 144.5 %all-reduce.7.cloned.1.call-done = (bf16[64,2304]{1,0:T(8,128)(2,1)}, bf16[32,2304]{1,0:T(8,128)(2,1)}) async-done(((bf16[64,2304]{1,0:T(8,128)(2,1)}, bf16[32,2304]{1,0:T(8,128)(2,1)}), (bf16[64,2304]{1,0:T(8,128)(2,1)}, bf16[32,2304]{1,0:T(8,128)(2,1)})) %all-reduce.7.cloned.1.call-update) | async-done | bytes 442384
  475.1 2.1 fusion.143
  (181 shorter events, 45.2 us)
Async XLA Ops:
  7.2 254.4 %copy-start = (bf16[4,128,2304]{2,1,0:T(8,128)(2,1)S(1)}, bf16[4,128,2304]{2,1,0:T(8,128)(2,1)}, u32[]{:S(2)}) copy-start(bf16[4,128,2304]{2,1,0:T(8,128)(2,1)} %param.43) | copy-start | bytes 7077892
  7.2 6.5 %copy-start.6 = (bf16[64,2304]{1,0:T(8,128)(2,1)S(1)}, bf16[64,2304]{1,0:T(8,128)(2,1)}, u32[]{:S(2)}) copy-start(bf16[64,2304]{1,0:T(8,128)(2,1)} %param.22) | copy-start | bytes 884740
  7.2 6.5 %copy-start.14 = (f32[2304]{0:T(1024)S(1)}, f32[2304]{0:T(1024)}, u32[]{:S(2)}) copy-start(f32[2304]{0:T(1024)} %param.28) | copy-start | bytes 27652
  15.2 7.2 %copy-start.5 = (bf16[64,1,128,128]{3,2,1,0:T(8,128)(2,1)S(1)}, bf16[64,1,128,128]{3,2,1,0:T(8,128)(2,1)}, u32[]{:S(2)}) copy-start(bf16[64,1,128,128]{3,2,1,0:T(8,128)(2,1)} %param.24) | copy-start | bytes 6291460
  32.8 7.6 %copy-start.3 = (bf16[32,2304]{1,0:T(8,128)(2,1)S(1)}, bf16[32,2304]{1,0:T(8,128)(2,1)}, u32[]{:S(2)}) copy-start(bf16[32,2304]{1,0:T(8,128)(2,1)} %param.23) | copy-start | bytes 442372
  32.8 37.4 %all-to-all-start = ((bf16[64,1,128,128]{3,2,1,0:T(8,128)(2,1)}), bf16[64,1,128,128]{3,2,1,0:T(8,128)(2,1)}, u32[]{:S(2)}, u32[]{:S(2)}) async-start(bf16[64,1,128,128]{3,2,1,0:T(8,128)(2,1)} %fusion.25), calls=%async_computation.1 | async-start | bytes 4194304 | tf_op jit(solution)/shard_map/all_to_all | solution.py:214
  40.4 184.8 %all-reduce.9.cloned.1.call-start = ((), (), s32[]{:S(2)}) async-start(), calls=%async_computation.7 | async-start | bytes 884736 | tf_op jit(solution)/shard_map/psum | solution.py:72
  47.5 7.1 %copy-start.22 = (s32[256,8]{0,1:T(8,128)S(1)}, s32[256,8]{0,1:T(8,128)}, u32[]{:S(2)}) copy-start(s32[256,8]{0,1:T(8,128)} %param.27) | copy-start | bytes 24580
  47.5 11.7 %copy-start.20 = (s32[512,8]{0,1:T(8,128)S(1)}, s32[512,8]{0,1:T(8,128)}, u32[]{:S(2)}) copy-start(s32[512,8]{0,1:T(8,128)} %param.26) | copy-start | bytes 49156
  57.2 11.3 %copy-start.4 = (bf16[128,2304]{1,0:T(8,128)(2,1)S(1)}, bf16[128,2304]{1,0:T(8,128)(2,1)}, u32[]{:S(2)}) copy-start(bf16[128,2304]{1,0:T(8,128)(2,1)} %param.38) | copy-start | bytes 1769476
  63.2 18.4 %copy-start.9 = (s32[256,8]{1,0:T(8,128)}, s32[256,8]{1,0:T(8,128)S(1)}, u32[]{:S(2)}) copy-start(s32[256,8]{1,0:T(8,128)S(1)} %gather_fusion) | copy-start | bytes 24580
  66.0 7.6 %copy-start.28 = (pred[32]{0:T(512)(128)(4,1)S(1)}, pred[32]{0:T(512)(128)(4,1)}, u32[]{:S(2)}) copy-start(pred[32]{0:T(512)(128)(4,1)} %get-tuple-element.14) | copy-start | bytes 100
  80.2 148.1 %copy-start.31 = (f32[2304]{0:T(1024)S(1)}, f32[2304]{0:T(1024)}, u32[]{:S(2)}) copy-start(f32[2304]{0:T(1024)} %param.39) | copy-start | bytes 27652
  81.3 182.0 %all-gather.2.cloned.1.call-start = ((), (), s32[]{:S(2)}) async-start(), calls=%async_computation.3 | async-start | bytes 1327104 | tf_op jit(solution)/shard_map/all_gather | solution.py:143
  83.6 145.7 %copy-start.18 = (pred[8,4,8,64]{3,2,1,0:T(8,128)(4,1)}, pred[8,4,8,64]{3,2,1,0:T(8,128)(4,1)S(1)}, u32[]{:S(2)}) copy-start(pred[8,4,8,64]{3,2,1,0:T(8,128)(4,1)S(1)} %get-tuple-element.18) | copy-start | bytes 49156
  229.3 62.1 %reduce-scatter.5.cloned.1.call-start = ((), (), s32[]{:S(2)}) async-start(), calls=%async_computation.5 | async-start | bytes 663552 | tf_op jit(solution)/shard_map/reduce_scatter | solution.py:162
  250.0 8.2 %copy-start.13 = (s32[128,8]{1,0:T(8,128)S(1)}, s32[128,8]{1,0:T(8,128)}, u32[]{:S(2)}) copy-start(s32[128,8]{1,0:T(8,128)} %copy-done.12) | copy-start | bytes 12292
  250.0 8.2 %copy-start.25 = (s32[4]{0:T(128)S(1)}, s32[4]{0:T(128)}, u32[]{:S(2)}) copy-start(s32[4]{0:T(128)} %copy-done.24) | copy-start | bytes 52
  250.0 8.4 %copy-start.21 = (pred[8,4,4]{2,1,0:T(4,128)(4,1)S(1)}, pred[8,4,4]{2,1,0:T(4,128)(4,1)}, u32[]{:S(2)}) copy-start(pred[8,4,4]{2,1,0:T(4,128)(4,1)} %reduce_or.49) | copy-start | bytes 388
  263.3 64.1 %reduce-scatter.3.cloned.1.call-start = ((), (), s32[]{:S(2)}) async-start(), calls=%async_computation.4 | async-start | bytes 1327104 | tf_op jit(solution)/shard_map/reduce_scatter | solution.py:162
  265.1 15.8 %copy-start.10 = (s32[256,8]{1,0:T(8,128)S(1)}, s32[256,8]{1,0:T(8,128)}, u32[]{:S(2)}) copy-start(s32[256,8]{1,0:T(8,128)} %copy-done.9) | copy-start | bytes 24580
  265.1 15.8 %copy-start.26 = (s32[4]{0:T(128)S(1)}, s32[4]{0:T(128)}, u32[]{:S(2)}) copy-start(s32[4]{0:T(128)} %copy-done.24) | copy-start | bytes 52
  288.1 41.2 %copy-start.32 = (u32[256]{0:T(256)S(1)}, u32[256]{0:T(256)}, u32[]{:S(2)}) copy-start(u32[256]{0:T(256)} %constant.276) | copy-start | bytes 3076
  290.5 184.6 %all-reduce.7.cloned.1.call-start = ((), (), s32[]{:S(2)}) async-start(), calls=%async_computation.6 | async-start | bytes 884736
  (15 other events, 52.6 us)
Sparse Core Ops, SparseCore 0:
  81.5 143.7 all-reduce.8
  229.4 28.1 all-gather.1
  263.4 28.0 reduce-scatter.4
  294.0 33.3 reduce-scatter.2
  331.2 143.9 all-reduce.6
where the time goes:
time: 490 us; the launch traced here: 485 us
  waiting for transfers between devices  321 us (66%)
  matrix products  54 us (11%)
  local copies, waits for them, and re-layouts  43.3 us (9%)
  other arithmetic  24.7 us (5%)
  blocking collectives  18.7 us (4%)
  between operations  15.9 us (3%)
  starting transfers between devices  7.98 us (2%)
    unnamed x6, waiting for transfers between devices  145 us
    psum x1, waiting for transfers between devices, attend(): lax.psum(partial_value.astype(jnp.bfloat16), 'expert').astype(jnp.float32)  142 us
    reduce_scatter x2, waiting for transfers between devices, mixture(): lax.psum_scatter(results.reshape(per_group * lax.axis_size('dp'), feature...  34.3 us
    gather x6, local copies, waits for them, and re-layouts, slot_weights(): chosen = jnp.take_along_axis(scores, slot_routes, axis=-1)  24.1 us
    all_gather x1, blocking collectives, mixture(): gathered = lax.all_gather(sent_rows, 'dp', axis=0, tiled=True)  18.7 us
  transfers between devices with their start and end apart: 6, of which 4 were waited for; matrix products, arithmetic and copies ran while one was open for 16% of the time, Pallas kernels for 0%

commit v1 on v0

v1 whole, which is shorter than its diff:
```python
import functools

import jax
import jax.numpy as jnp
from jax import lax
from jax.experimental import pallas as pl
from jax.experimental.pallas import tpu as pltpu
from jax.sharding import PartitionSpec as P

F32 = jnp.float32
BF16 = jnp.bfloat16
EPS = 1e-06
ROUTE_SCALE = 2.446
MESH = pl.DeviceIdType.MESH
VMEM_LIMIT = 48 * 1024 * 1024
D = 2304
H = 128
NCT = D // 128
R1 = 64
R2 = 32
RT = R1 + R2
SLOTS = 48
NE = 32
ND = 8
NOWN = 27


def iota(shape, dim):
    return lax.broadcasted_iota(jnp.int32, shape, dim)


def dot(a, b, contract=((1,), (0,)), precision=None):
    return lax.dot_general(
        a, b, (contract, ((), ())), precision=precision, preferred_element_type=F32
    )


def rms(wide, gain):
    factor = lax.rsqrt(jnp.mean(wide * wide, axis=-1, keepdims=True) + EPS)
    return wide * factor * gain


def rcopy(src, dst, send, recv, axis, index):
    return pltpu.make_async_remote_copy(
        src_ref=src,
        dst_ref=dst,
        send_sem=send,
        recv_sem=recv,
        device_id={axis: index},
        device_id_type=MESH,
    )


def greet(axes):
    barrier = pltpu.get_barrier_semaphore()
    total = 0
    for axis, size in axes:
        me = lax.axis_index(axis)

        def tell(k, carry):
            pl.semaphore_signal(
                barrier,
                inc=1,
                device_id={axis: lax.rem(me + k, size)},
                device_id_type=MESH,
            )
            return carry

        lax.fori_loop(1, size, tell, 0)
        total += size - 1
    pl.semaphore_wait(barrier, total)


def project_kernel(
    x1, x2, gain, wq, wk, wv, wdd, wdu, bias, dlog, wb, p1, p2, normed
):
    normed[0:R1, :] = rms(x1[...].astype(F32), gain[...]).astype(BF16)
    normed[R1:RT, :] = rms(x2[...].astype(F32), gain[...]).astype(BF16)
    n = normed[...]

    def project(w):
        produced = dot(n, w[...])
        return produced * jax.nn.sigmoid(produced)

    def unit(v):
        return v * lax.rsqrt(jnp.sum(v * v, axis=-1, keepdims=True) + EPS)

    q = unit(project(wq))
    k = unit(project(wk))
    v = project(wv)
    low = dot(n, wdd[...]).astype(BF16)
    gate = dot(low, wdu[...]) + bias[...]
    soft = jnp.maximum(gate, 0.0) + jnp.log(1.0 + jnp.exp(-jnp.abs(gate)))
    strength = jnp.exp(jnp.full((RT, H), dlog[0], F32))
    decay = jnp.exp(-(strength * soft))
    beta = jax.nn.sigmoid(
        jnp.sum(n.astype(F32) * wb[...].astype(F32), axis=-1, keepdims=True)
    )
    dk = decay * k
    dq = decay * q
    s = jnp.broadcast_to(beta * jnp.sum(k * q, axis=-1, keepdims=True), (RT, H))
    dk_hi = dk.astype(BF16).astype(F32)
    dq_hi = dq.astype(BF16).astype(F32)
    parts = (dk_hi, dk - dk_hi, dq_hi, dq - dq_hi, v, s, decay, beta * k)
    for c, part in enumerate(parts):
        p1[:, c * H : (c + 1) * H] = part[0:R1, :]
    for c, part in enumerate((dk, dq, v, s)):
        p2[:, c * H : (c + 1) * H] = part[R1:RT, :].astype(BF16)


def share_kernel(p2, out, send, recv, local):
    me = lax.axis_index("dp")
    greet((("dp", ND),))
    own = pltpu.make_async_copy(p2, out.at[me], local)
    own.start()

    def start(k, carry):
        peer = lax.rem(me + k, ND)
        rcopy(p2, out.at[me], send.at[peer], recv.at[me], "dp", peer).start()
        return carry

    def finish(k, carry):
        peer = lax.rem(me + k, ND)
        copy = rcopy(p2, out.at[peer], send.at[peer], recv.at[peer], "dp", peer)
        copy.wait_send()
        copy.wait_recv()
        return carry

    lax.fori_loop(1, ND, start, 0)
    lax.fori_loop(1, ND, finish, 0)
    own.wait()


def attend_kernel(p1, p2, st, ids, og, h1, h2, named, tp, h1s, h2s, ro1, ro2):
    i = pl.program_id(0)

    @pl.when(i == 0)
    def _():
        base = lax.axis_index("dp") * R1
        named[...] = (ids[...] == base + iota((R1, 256), 0)).astype(F32)
        tp[...] = dot(named[...].astype(BF16), p2[...])

    m = iota((16, H), 0)
    t2 = tp[pl.ds(pl.multiple_of(i * 8, 8), 8), :]
    dcol = jnp.transpose(p1[:, 6 * H : 7 * H])
    bcol = jnp.transpose(p1[:, 7 * H : 8 * H])
    for j in range(8):

        def row(c):
            return p1[j : j + 1, c * H : (c + 1) * H]

        def row2(c):
            return t2[j : j + 1, c * H : (c + 1) * H]

        state = st[j]
        a = jnp.where(m == 0, row(0), jnp.where(m == 1, row(1), jnp.where(m == 2, row(2), row(3))))
        got = dot(a.astype(BF16), state)
        u = row(4) - (got[0:1] + got[1:2])
        ro1[j : j + 1, :] = got[2:3] + got[3:4] + row(5) * u
        fresh = state.astype(F32) * dcol[:, j : j + 1] + bcol[:, j : j + 1] * u
        a2 = jnp.where(m == 0, row2(0), row2(1))
        got2 = dot(a2.astype(BF16), fresh.astype(BF16))
        u2 = row2(2) - got2[0:1]
        ro2[j : j + 1, :] = got2[1:2] + row2(3) * u2
    rows = pl.ds(pl.multiple_of(i * 8, 8), 8)
    h1s[rows, :] = rms(ro1[...] * H**-0.5, og[...])
    h2s[rows, :] = rms(ro2[...] * H**-0.5, og[...])

    @pl.when(i == pl.num_programs(0) - 1)
    def _():
        h1[...] = h1s[...].astype(BF16)
        h2[...] = dot(
            named[...].astype(BF16), h2s[...].astype(BF16), ((0,), (0,))
        ).astype(BF16)


def hidden_kernel(
    h1, h2, wo, x1, x2, gain, router, routes1, routes2,
    slots, hid, share_w,
    h2r, rs_send, rs_recv, ag_send, ag_recv, xt, pick,
    hs, hr, as_, ar, bs, br, cs, cr, local,
):
    dp = lax.axis_index("dp")
    ex = lax.axis_index("expert")
    y = dp // 2
    core = lax.rem(dp, 2)
    greet((("dp", ND), ("expert", NE)))

    def h_copy(peer, slot):
        return rcopy(h2.at[peer], h2r.at[slot], hs.at[peer], hr.at[slot], "dp", peer)

    def h_start(k, carry):
        h_copy(lax.rem(dp + k, ND), dp).start()
        return carry

    def h_wait(k, carry):
        peer = lax.rem(dp + k, ND)
        h_copy(peer, peer).wait_recv()
        return carry

    def h_sent(k, carry):
        peer = lax.rem(dp + k, ND)
        h_copy(peer, peer).wait_send()
        return carry

    lax.fori_loop(1, ND, h_start, 0)

    order = iota((R1, R1), 0)
    source = jnp.where(order < 32, 2 * order, 2 * (order - 32) + 1)
    perm = (iota((R1, R1), 1) == source).astype(BF16)
    heads1 = dot(perm, h1[...]).astype(BF16)
    part1 = dot(heads1, wo[...])
    for ct in range(NCT):
        for rb in range(4):
            t = ct * 6 + rb
            rs_send[t // 4, t % 4] = part1[
                rb * 16 : rb * 16 + 16, ct * 128 : ct * 128 + 128
            ].astype(BF16)
    xp = dot(perm, x1[...]).astype(BF16)
    for ct in range(NCT):
        for rb in range(6):
            src = xp[rb * 16 : rb * 16 + 16, ct * 128 : ct * 128 + 128] if rb < 4 else x2[(rb - 4) * 16 : (rb - 4) * 16 + 16, ct * 128 : ct * 128 + 128]
            xt[ct * 6 + rb] = src

    lanes = iota((R1, 128), 1)
    tab1 = routes1[pl.ds(pl.multiple_of(dp * R1, R1), R1), :]
    tab2 = routes2[pl.ds(pl.multiple_of(dp * R2, R2), R2), :]

    def multi_hot(tab, rows):
        hot = jnp.zeros((rows, 128), F32)
        for k in range(8):
            hot = hot + (tab[:, k : k + 1] == lanes[0:rows]).astype(F32)
        return hot

    mask1 = dot(perm, multi_hot(tab1, R1).astype(BF16))
    mask2 = multi_hot(tab2, R2)
    tri = (iota((R1, R1), 0) >= iota((R1, R1), 1)).astype(BF16)
    rank1 = mask1 * dot(tri, mask1.astype(BF16))
    rank2 = mask2 * dot(tri[0:R2, 0:R2], mask2.astype(BF16))
    mask = jnp.concatenate([mask1, mask2], axis=0)
    rank = jnp.concatenate([rank1, rank2], axis=0).astype(BF16)

    def expert_of(s):
        return 4 * ex + jnp.where(s < 32, s >> 3, (s - 32) >> 2)

    def place_of(s):
        return jnp.where(s < 32, s & 7, (s - 32) & 3) + 1

    ex_a = (iota((128, SLOTS), 0) == expert_of(iota((128, SLOTS), 1))).astype(F32)
    ex_b = (iota((SLOTS, 128), 1) == expert_of(iota((SLOTS, 128), 0))).astype(BF16)
    place_a = place_of(iota((RT, SLOTS), 1)).astype(F32)
    place_b = place_of(iota((SLOTS, RT), 0)).astype(F32)
    kind_a = (iota((RT, SLOTS), 0) < R1) == (iota((RT, SLOTS), 1) < 32)
    kind_b = (iota((SLOTS, RT), 1) < R1) == (iota((SLOTS, RT), 0) < 32)
    sel_a = jnp.where(kind_a & (dot(rank, ex_a.astype(BF16)) == place_a), 1.0, 0.0)
    sel_b = jnp.where(kind_b & (dot(ex_b, rank, ((1,), (1,))) == place_b), 1.0, 0.0)

    lax.fori_loop(1, ND, h_wait, 0)
    h2r[dp] = h2[dp]
    heads2 = h2r[0].astype(F32)
    for g in range(1, ND):
        heads2 = heads2 + h2r[g].astype(F32)
    part2 = dot(heads2.astype(BF16), wo[...])
    for ct in range(NCT):
        for rb in range(2):
            t = ct * 6 + 4 + rb
            rs_send[t // 4, t % 4] = part2[
                rb * 16 : rb * 16 + 16, ct * 128 : ct * 128 + 128
            ].astype(BF16)

    def a_copy(peer, slot):
        return rcopy(rs_send.at[peer], rs_recv.at[slot], as_.at[peer], ar.at[slot], "expert", peer)

    def a_start(k, carry):
        peer = lax.rem(ex + k, NE)

        @pl.when(peer < NOWN)
        def _():
            a_copy(peer, ex).start()

        return carry

    def a_sent(k, carry):
        peer = lax.rem(ex + k, NE)

        @pl.when(peer < NOWN)
        def _():
            a_copy(peer, ex).wait_send()

        return carry

    def a_wait(k, carry):
        a_copy(lax.rem(ex + NE - k, NE), lax.rem(ex + NE - k, NE)).wait_recv()
        return carry

    def b_copy(peer, slot):
        return rcopy(ag_send, ag_recv.at[slot], bs.at[peer], br.at[slot], "expert", peer)

    def b_start(k, carry):
        b_copy(lax.rem(ex + k, NE), ex).start()
        return carry

    def b_sent(k, carry):
        b_copy(lax.rem(ex + k, NE), ex).wait_send()
        return carry

    def b_wait(k, carry):
        peer = lax.rem(ex + NE - k, NE)

        @pl.when(peer < NOWN)
        def _():
            b_copy(peer, peer).wait_recv()

        return carry

    lax.fori_loop(1, NE, a_start, 0)

    @pl.when(ex < NOWN)
    def _():
        rs_recv[ex] = rs_send[ex]
        lax.fori_loop(1, NE, a_wait, 0)

        def add(s, total):
            return total + rs_recv[s].astype(F32)

        total = lax.fori_loop(0, NE, add, jnp.zeros((4, 16, 128), F32))
        total = total + xt[pl.ds(4 * ex, 4)].astype(F32)
        ag_send[...] = total.astype(BF16)
        ag_recv[ex] = ag_send[...]
        lax.fori_loop(1, NE, b_start, 0)

    lax.fori_loop(1, NE, b_wait, 0)
    for ct in range(NCT):
        for rb in range(6):
            t = ct * 6 + rb
            hid[rb * 16 : rb * 16 + 16, ct * 128 : ct * 128 + 128] = ag_recv[t // 4, t % 4]
    normed = rms(hid[...].astype(F32), gain[...]).astype(BF16)
    pick[...] = dot(sel_b.astype(BF16), normed).astype(BF16)

    def c_copy(src, slot, peer, sem):
        return rcopy(src, slots.at[slot], cs.at[sem], cr.at[slot], "dp", peer)

    def same(s):
        return 2 * lax.rem(y + s, 4) + core

    def sib(s):
        return 2 * lax.rem(y + s, 4) + 1 - core

    sibling = sib(0)
    for s in (2, 1, 3):
        c_copy(pick, dp, same(s), s).start()
    c_copy(pick, dp, sibling, 0).start()
    own = pltpu.make_async_copy(pick, slots.at[dp], local)
    own.start()

    logits = dot(normed, router[...])
    scores = jax.nn.sigmoid(logits) * mask
    shares = ROUTE_SCALE * scores / jnp.sum(scores, axis=-1, keepdims=True)
    share_w[...] = dot(shares, ex_a, precision=lax.Precision.HIGHEST) * sel_a

    for s in (1, 3, 2):
        c_copy(pick, same(s), same(s), s).wait_recv()
        c_copy(slots.at[same(s)], same(s), sibling, 3 + s).start()
    own.wait()
    for s in (0, 1, 3, 2):
        c_copy(pick, sib(s), sibling, 0).wait_recv()
    for s in (0, 1, 2, 3):
        c_copy(pick, dp, sibling, s).wait_send()
    for s in (1, 2, 3):
        c_copy(slots.at[same(s)], same(s), sibling, 3 + s).wait_send()
    lax.fori_loop(1, ND, h_sent, 0)
    lax.fori_loop(1, NE, a_sent, 0)

    @pl.when(ex < NOWN)
    def _():
        lax.fori_loop(1, NE, b_sent, 0)


def expert_kernel(slots, wg, wu, wd, out, acc):
    e = pl.program_id(0)
    pair = e // 2

    @pl.when(e == 0)
    def _():
        acc[...] = jnp.zeros_like(acc)

    def apply(rows, mine):
        x = slots[:, rows, :].reshape(ND * 16, D)
        g = dot(x, wg[0])
        u = dot(x, wu[0])
        active = g * jax.nn.sigmoid(g) * u
        place = iota((ND * 16, H), 0) & 15
        active = jnp.where(mine(place), active, 0.0).astype(BF16)
        acc[:, rows, :] += dot(active, wd[0]).reshape(ND, 16, D)

    apply(pl.ds(pl.multiple_of(16 * pair, 16), 16), lambda p: (p >> 3) == e - 2 * pair)
    apply(pl.ds(32, 16), lambda p: (p >> 2) == e)

    @pl.when(e == pl.num_programs(0) - 1)
    def _():
        out[...] = acc[...].astype(BF16)


def combine_kernel(
    out, hid, share_w, first, tail,
    pr, z, zr, scr, e_send, e_recv, rows,
    ps, prs, zs, zrs, es, er,
):
    dp = lax.axis_index("dp")
    ex = lax.axis_index("expert")
    y = dp // 2
    core = lax.rem(dp, 2)
    greet((("dp", ND), ("expert", NE)))

    def p_copy(yy):
        return rcopy(out.at[2 * yy + 1 - core], pr.at[yy], ps.at[yy], prs.at[yy], "dp", 2 * y + 1 - core)

    def z_copy(s, slot):
        yy = lax.rem(y + s, 4)
        return rcopy(z.at[yy], zr.at[slot], zs.at[yy], zrs.at[slot], "dp", 2 * yy + core)

    for s in (2, 1, 3, 0):
        p_copy(lax.rem(y + s, 4)).start()
    for s in (2, 1, 3):
        yy = lax.rem(y + s, 4)
        p_copy(yy).wait_recv()
        z[yy] = (out[2 * yy + core].astype(F32) + pr[yy].astype(F32)).astype(BF16)
        z_copy(s, y).start()
    p_copy(y).wait_recv()
    total = out[dp].astype(F32) + pr[y].astype(F32)
    for s in (1, 3, 2):
        yy = lax.rem(y + s, 4)
        z_copy(s, yy).wait_recv()
        total = total + zr[yy].astype(F32)
    summed = total.astype(BF16)
    w = share_w[...]
    w_hi = w.astype(BF16)
    w_lo = (w - w_hi.astype(F32)).astype(BF16)
    r = iota((RT, RT), 0)
    mine = ((r == iota((RT, RT), 1)) & ((r & 31) == ex)).astype(BF16)
    res = dot(w_hi, summed) + dot(w_lo, summed) + dot(mine, hid[...])
    for ct in range(NCT):
        for j in range(3):
            scr[pl.ds(j * NCT + ct, NE, stride=64), :] = res[
                j * 32 : j * 32 + 32, ct * 128 : ct * 128 + 128
            ]
    for c in range(NE):
        e_send[c] = scr[c * 64 : c * 64 + 64, :].astype(BF16)

    def e_copy(peer, slot):
        return rcopy(e_send.at[peer], e_recv.at[slot], es.at[peer], er.at[slot], "expert", peer)

    def e_start(k, carry):
        e_copy(lax.rem(ex + k, NE), ex).start()
        return carry

    def e_wait(k, carry):
        peer = lax.rem(ex + NE - k, NE)
        e_copy(peer, peer).wait_recv()
        return carry

    def e_sent(k, carry):
        e_copy(lax.rem(ex + k, NE), ex).wait_send()
        return carry

    lax.fori_loop(1, NE, e_start, 0)
    e_recv[ex] = jnp.zeros((64, 128), BF16)
    lax.fori_loop(1, NE, e_wait, 0)

    def add(s, total):
        return total + e_recv[s].astype(F32)

    total = scr[pl.ds(pl.multiple_of(ex * 64, 64), 64), :]
    total = lax.fori_loop(0, NE, add, total)
    for j in range(3):
        for ct in range(NCT):
            at = j * NCT + ct
            rows[j : j + 1, ct * 128 : ct * 128 + 128] = total[at : at + 1, :]
    first[...] = rows[0:2, :].astype(BF16)
    tail[...] = rows[2:3, :].astype(BF16)
    lax.fori_loop(1, NE, e_sent, 0)
    for s in (0, 1, 2, 3):
        p_copy(lax.rem(y + s, 4)).wait_send()
    for s in (1, 2, 3):
        z_copy(s, y).wait_send()


def params(collective_id=None):
    if collective_id is None:
        return pltpu.CompilerParams(vmem_limit_bytes=VMEM_LIMIT)
    return pltpu.CompilerParams(
        vmem_limit_bytes=VMEM_LIMIT, collective_id=collective_id, has_side_effects=True
    )


VM = pl.BlockSpec(memory_space=pltpu.VMEM)
SM = pl.BlockSpec(memory_space=pltpu.SMEM)
DMA = pltpu.SemaphoreType.DMA


def shape(dims, dtype):
    return jax.ShapeDtypeStruct(dims, dtype)


def on_device(
    inputs, tail_inputs, states, tail_ids, routes, tail_routes, attention_gain,
    query_weight, key_weight, value_weight, decay_down, decay_up, decay_bias,
    decay_log, beta_weight, output_gain, head_out, expert_gain, router_weight,
    gate_weight, up_weight, down_weight,
):
    p1, p2 = pl.pallas_call(
        project_kernel,
        out_shape=(shape((R1, 8 * H), F32), shape((R2, 4 * H), BF16)),
        in_specs=[VM] * 9 + [SM, VM],
        out_specs=(VM, VM),
        scratch_shapes=[pltpu.VMEM((RT, D), BF16)],
        compiler_params=params(),
        name="project",
    )(
        inputs, tail_inputs, attention_gain.reshape(1, D), query_weight, key_weight,
        value_weight, decay_down, decay_up, decay_bias.reshape(1, H), decay_log,
        beta_weight.reshape(1, D),
    )
    p2all = pl.pallas_call(
        share_kernel,
        out_shape=shape((ND, R2, 4 * H), BF16),
        in_specs=[VM],
        out_specs=VM,
        scratch_shapes=[DMA((ND,)), DMA((ND,)), DMA],
        compiler_params=params(0),
        name="share_rows",
    )(p2)
    h1, h2 = pl.pallas_call(
        attend_kernel,
        grid=(8,),
        out_shape=(shape((R1, H), BF16), shape((ND * R2, H), BF16)),
        in_specs=[
            pl.BlockSpec((8, 8 * H), lambda i: (i, 0)),
            pl.BlockSpec((ND * R2, 4 * H), lambda i: (0, 0)),
            pl.BlockSpec((8, H, H), lambda i: (i, 0, 0)),
            pl.BlockSpec((1, 256), lambda i: (0, 0)),
            pl.BlockSpec((1, H), lambda i: (0, 0)),
        ],
        out_specs=(
            pl.BlockSpec((R1, H), lambda i: (0, 0)),
            pl.BlockSpec((ND * R2, H), lambda i: (0, 0)),
        ),
        scratch_shapes=[
            pltpu.VMEM((R1, 256), F32),
            pltpu.VMEM((R1, 4 * H), F32),
            pltpu.VMEM((R1, H), F32),
            pltpu.VMEM((R1, H), F32),
            pltpu.VMEM((8, H), F32),
            pltpu.VMEM((8, H), F32),
        ],
        compiler_params=params(),
        name="attend",
    )(
        p1, p2all.reshape(ND * R2, 4 * H), states.reshape(R1, H, H),
        tail_ids.reshape(1, 256), output_gain.reshape(1, H),
    )
    slots, hid, share_w = pl.pallas_call(
        hidden_kernel,
        out_shape=(
            shape((ND, SLOTS, D), BF16),
            shape((RT, D), BF16),
            shape((RT, SLOTS), F32),
        ),
        in_specs=[VM] * 9,
        out_specs=(VM, VM, VM),
        scratch_shapes=[
            pltpu.VMEM((ND, R2, H), BF16),
            pltpu.VMEM((NE, 4, 16, 128), BF16),
            pltpu.VMEM((NE, 4, 16, 128), BF16),
            pltpu.VMEM((4, 16, 128), BF16),
            pltpu.VMEM((NE, 4, 16, 128), BF16),
            pltpu.VMEM((NE * 4, 16, 128), BF16),
            pltpu.VMEM((SLOTS, D), BF16),
            DMA((ND,)), DMA((ND,)),
            DMA((NE,)), DMA((NE,)),
            DMA((NE,)), DMA((NE,)),
            DMA((ND,)), DMA((ND,)),
            DMA,
        ],
        compiler_params=params(1),
        name="hidden",
    )(
        h1, h2.reshape(ND, R2, H), head_out, inputs, tail_inputs,
        expert_gain.reshape(1, D), router_weight, routes, tail_routes,
    )
    out = pl.pallas_call(
        expert_kernel,
        grid=(4,),
        out_shape=shape((ND, SLOTS, D), BF16),
        in_specs=[
            pl.BlockSpec((ND, SLOTS, D), lambda e: (0, 0, 0)),
            pl.BlockSpec((1, D, H), lambda e: (e, 0, 0)),
            pl.BlockSpec((1, D, H), lambda e: (e, 0, 0)),
            pl.BlockSpec((1, H, D), lambda e: (e, 0, 0)),
        ],
        out_specs=pl.BlockSpec((ND, SLOTS, D), lambda e: (0, 0, 0)),
        scratch_shapes=[pltpu.VMEM((ND, SLOTS, D), F32)],
        compiler_params=params(),
        name="experts",
    )(slots, gate_weight, up_weight, down_weight)
    return pl.pallas_call(
        combine_kernel,
        out_shape=(shape((2, D), BF16), shape((1, D), BF16)),
        in_specs=[VM] * 3,
        out_specs=(VM, VM),
        scratch_shapes=[
            pltpu.VMEM((4, SLOTS, D), BF16),
            pltpu.VMEM((4, SLOTS, D), BF16),
            pltpu.VMEM((4, SLOTS, D), BF16),
            pltpu.VMEM((NE * 64, 128), F32),
            pltpu.VMEM((NE, 64, 128), BF16),
            pltpu.VMEM((NE, 64, 128), BF16),
            pltpu.VMEM((8, D), F32),
            DMA((4,)), DMA((4,)),
            DMA((4,)), DMA((4,)),
            DMA((NE,)), DMA((NE,)),
        ],
        compiler_params=params(2),
        name="combine",
    )(out, hid, share_w)


def solution(mesh):
    placed = (
        P("dp", None),
        P("dp", None),
        P("dp", "expert", None, None),
        P(),
        P(),
        P(),
        P(),
        P(None, "expert"),
        P(None, "expert"),
        P(None, "expert"),
        P(),
        P(None, "expert"),
        P("expert"),
        P("expert"),
        P(None, "expert"),
        P(),
        P("expert", None),
        P(),
        P(),
        P("expert", None, "dp"),
        P("expert", None, "dp"),
        P("expert", "dp", None),
    )
    return jax.shard_map(
        on_device,
        mesh=mesh,
        in_specs=placed,
        out_specs=(P(("dp", "expert"), None), P(("dp", "expert"), None)),
        check_vma=False,
    )
```

time: 490 us -> 130 us (0.27)
  waiting for transfers between devices: 321 us -> 0 us
  Pallas kernels: 0 us -> 116 us
  matrix products: 54 us -> 0 us
  local copies, waits for them, and re-layouts: 43.3 us -> 12.6 us
  other arithmetic: 24.7 us -> 0 us
  blocking collectives: 18.7 us -> 0 us
  between operations: 15.9 us -> 1.59 us
  starting transfers between devices: 7.98 us -> 0 us
    unnamed x6 -> x0, waiting for transfers between devices: 145 us -> none
    psum x1 -> x0, waiting for transfers between devices: 142 us -> none  [attend(): lax.psum(partial_value.astype(jnp.bfloat16), 'expert').astype(jnp.float32)]
    pallas_call x0 -> x6, Pallas kernels: none -> 116 us  [the longest x1 54.3 us: on_device(): pl.pallas_call(hidden_kernel, out_shape=(shape((ND, SLOTS, D), BF16), sha...]
    dot_general x27 -> x0, matrix products: 54 us -> none  [the longest x6 9.42 us: project(): produced = jnp.dot(normed, weight, preferred_element_type=jnp.float32)]
    reduce_scatter x2 -> x0, waiting for transfers between devices: 34.3 us -> none  [mixture(): lax.psum_scatter(results.reshape(per_group * lax.axis_size('dp'), feature...]
    gather x10 -> x0, local copies, waits for them, and re-layouts: 34.2 us -> none  [the longest x6 24.1 us: slot_weights(): chosen = jnp.take_along_axis(scores, slot_routes, axis=-1)]
    all_gather x1 -> x0, blocking collectives: 18.7 us -> none  [mixture(): gathered = lax.all_gather(sent_rows, 'dp', axis=0, tiled=True)]
    unnamed x70 -> x36, local copies, waits for them, and re-layouts: 2.35 us -> 11.1 us
  transfers between devices with their start and end apart: 6 -> 0, of which waited for: 4 -> 0; matrix products, arithmetic and copies ran while one was open for 16% -> 0% of each run, Pallas kernels for 0% -> 0%
where the time goes in v1:
time: 130 us
  Pallas kernels  116 us (89%)
  local copies, waits for them, and re-layouts  12.6 us (10%)
  between operations  1.59 us (1%)
    pallas_call x1, Pallas kernels, on_device(): pl.pallas_call(hidden_kernel, out_shape=(shape((ND, SLOTS, D), BF16), sha...  54.3 us
    pallas_call x1, Pallas kernels, on_device(): pl.pallas_call(combine_kernel, out_shape=(shape((2, D), BF16), shape((1,...  36.7 us
    unnamed x36, local copies, waits for them, and re-layouts  11.1 us
    pallas_call x1, Pallas kernels, on_device(): pl.pallas_call(share_kernel, out_shape=shape((ND, R2, 4 * H), BF16), in_s...  10.3 us
    pallas_call x1, Pallas kernels, on_device(): pl.pallas_call(expert_kernel, grid=(4,), out_shape=shape((ND, SLOTS, D),...  7.12 us
    pallas_call x1, Pallas kernels, on_device(): pl.pallas_call(attend_kernel, grid=(8,), out_shape=(shape((R1, H), BF16),...  6.33 us

profile of v1, /device:TPU:1, one launch (start us, length us, event | category | flops | bytes accessed | tf_op | source)
XLA Modules:
  0.0 129.8 jit_solution(852611034429789268)
XLA Ops:
  1.4 0.7 reshape.31.gain
  2.1 0.7 reshape.39.gain
  2.9 0.8 copy.25.routes2
  3.7 0.8 copy.24.routes1
  4.5 0.0 copy-start.2
  4.6 1.0 copy-done.2
  5.5 1.1 copy-done.4
  6.6 1.1 copy-done.5
  7.6 1.1 copy-done.6
  8.7 1.1 copy-done.7
  9.8 0.9 copy-done.10
  10.7 0.8 copy-done.11
  11.4 0.7 copy-done.12
  12.1 0.7 copy-done.14
  12.8 0.0 copy-start.9
  12.8 1.0 project.1
  13.8 10.3 %share_rows.1 = bf16[8,32,512]{2,1,0:T(8,128)(2,1)S(1)} custom-call(bf16[32,512]{1,0:T(8,128)(2,1)S(1)} %get-tuple-element.10.p2), custom_call_target="tpu_custom_call" | custom-call | tf_op jit(solution)/shard_map/share_rows/pallas_call | solution.py:524
  24.1 0.0 copy-start
  24.1 6.3 %attend.1 = (bf16[64,128]{1,0:T(8,128)(2,1)S(1)}, bf16[256,128]{1,0:T(8,128)(2,1)S(1)}) custom-call(f32[64,1024]{1,0:T(8,128)S(1)} %get-tuple-element.9.p1, bf16[256,512]{1,0:T(8,128)(2,1)S(1)} %bitcast.8, bf16[64,128,128]{2,1,0:T(8,128)(2,1)S(1)} %bitcast.7, s32[1,256]{1,0:T(1,128)S(1)} %bitcast.11, f32[1,128]{1,0:T(1,128)S(1)} %bitcast.13), custom_call_target="tpu_custom_call" | custom-call | tf_op jit(solution)/shard_map/attend/pallas_call | solution.py:533
  30.5 54.3 %hidden.1 = (bf16[8,48,2304]{2,1,0:T(8,128)(2,1)S(1)}, bf16[96,2304]{1,0:T(8,128)(2,1)S(1)}, f32[96,48]{1,0:T(8,128)S(1)}) custom-call(bf16[64,128]{1,0:T(8,128)(2,1)S(1)} %get-tuple-element.11.h1, bf16[8,32,128]{2,1,0:T(8,128)(2,1)S(1)} %bitcast.9, bf16[128,2304]{1,0:T(8,128)(2,1)S(1)} %copy-done.8, bf16[64,2304]{1,0:T(8,128)(2,1)S(1)} %copy-done.3, ...), custom_call_target="tpu_custom_call" | custom-call | tf_op jit(solution)/shard_map/hidden/pallas_call | solution.py:562
  84.8 7.1 %experts.1.out = bf16[8,48,2304]{2,1,0:T(8,128)(2,1)S(1)} custom-call(bf16[8,48,2304]{2,1,0:T(8,128)(2,1)S(1)} %get-tuple-element.13.slots, bf16[4,2304,128]{2,1,0:T(8,128)(2,1)S(1)} %copy-done, bf16[4,2304,128]{2,1,0:T(8,128)(2,1)} %wu.1, bf16[4,128,2304]{2,1,0:T(8,128)(2,1)} %wd.1), custom_call_target="tpu_custom_call" | custom-call | tf_op jit(solution)/shard_map/experts/pallas_call | solution.py:591
  91.9 36.7 %combine.1 = (bf16[2,2304]{1,0:T(2,128)(2,1)S(1)}, bf16[1,2304]{1,0:T(2,128)(2,1)S(1)}) custom-call(bf16[8,48,2304]{2,1,0:T(8,128)(2,1)S(1)} %experts.1.out, bf16[96,2304]{1,0:T(8,128)(2,1)S(1)} %get-tuple-element.14.hid, f32[96,48]{1,0:T(8,128)S(1)} %get-tuple-element.15.share_w), custom_call_target="tpu_custom_call" | custom-call | tf_op jit(solution)/shard_map/combine/pallas_call | solution.py:606
  128.6 0.6 copy.29
  129.2 0.6 copy.30
  (20 shorter events, 0.0 us)
Async XLA Ops:
  0.6 23.4 %copy-start.1 = (bf16[64,1,128,128]{3,2,1,0:T(8,128)(2,1)S(1)}, bf16[64,1,128,128]{3,2,1,0:T(8,128)(2,1)}, u32[]{:S(2)}) copy-start(bf16[64,1,128,128]{3,2,1,0:T(8,128)(2,1)} %param.24) | copy-start | bytes 6291460
  4.5 1.0 copy-start.2
  5.5 1.1 copy-start.4
  6.6 1.1 copy-start.5
  7.6 1.1 copy-start.6
  8.7 1.1 copy-start.7
  9.8 0.9 copy-start.10
  10.7 0.8 copy-start.11
  11.4 0.7 copy-start.12
  12.1 0.7 copy-start.14
  12.8 11.3 %copy-start.13 = (s32[256]{0:T(256)S(1)}, s32[256]{0:T(256)}, u32[]{:S(2)}) copy-start(s32[256]{0:T(256)} %param.25) | copy-start | bytes 3076
  12.8 11.3 %copy-start.15 = (f32[128]{0:T(128)S(1)}, f32[128]{0:T(128)}, u32[]{:S(2)}) copy-start(f32[128]{0:T(128)} %param.37) | copy-start | bytes 1540
  12.8 17.7 %copy-start.3 = (bf16[64,2304]{1,0:T(8,128)(2,1)S(1)}, bf16[64,2304]{1,0:T(8,128)(2,1)}, u32[]{:S(2)}) copy-start(bf16[64,2304]{1,0:T(8,128)(2,1)} %x1.3) | copy-start | bytes 884740
  12.8 17.7 %copy-start.8 = (bf16[128,2304]{1,0:T(8,128)(2,1)S(1)}, bf16[128,2304]{1,0:T(8,128)(2,1)}, u32[]{:S(2)}) copy-start(bf16[128,2304]{1,0:T(8,128)(2,1)} %wo.1) | copy-start | bytes 1769476
  12.8 17.7 %copy-start.9 = (bf16[2304,128]{1,0:T(8,128)(2,1)S(1)}, bf16[2304,128]{1,0:T(8,128)(2,1)}, u32[]{:S(2)}) copy-start(bf16[2304,128]{1,0:T(8,128)(2,1)} %router.1) | copy-start | bytes 1769476
  24.1 60.7 %copy-start = (bf16[4,2304,128]{2,1,0:T(8,128)(2,1)S(1)}, bf16[4,2304,128]{2,1,0:T(8,128)(2,1)}, u32[]{:S(2)}) copy-start(bf16[4,2304,128]{2,1,0:T(8,128)(2,1)} %wg.1) | copy-start | bytes 7077892

commit v2 on v0

v2 whole, which is shorter than its diff:
```python
import jax
import jax.numpy as jnp
from jax import lax
from jax.experimental import pallas as pl
from jax.experimental.pallas import tpu as pltpu
from jax.sharding import PartitionSpec as P

F32 = jnp.float32
BF16 = jnp.bfloat16
EPS = 1e-06
ROUTE_SCALE = 2.446
MESH = pl.DeviceIdType.MESH
VMEM_LIMIT = 56 * 1024 * 1024
D = 2304
H = 128
NCT = D // 128
R1 = 64
R2 = 32
RT = R1 + R2
ND = 8
NX = 4
NZ = 8
ROWS = (64, 32)
SLOTS = (32, 16)
TILES = (18, 9)
OWNERS = (6, 3)
OUTS = (48, 32)
AX, AZ, BZ, BX, CC, DP, DY, EX, EZ = range(0, 18, 2)
KINDS = 18
PACK, HEAD = 2 * KINDS, 2 * KINDS + 2
SEM_ROWS = 2 * KINDS + 4


def iota(shape, dim):
    return lax.broadcasted_iota(jnp.int32, shape, dim)


def dot(a, b, contract=((1,), (0,)), precision=None):
    return lax.dot_general(
        a, b, (contract, ((), ())), precision=precision, preferred_element_type=F32
    )


def rms(wide, gain):
    factor = lax.rsqrt(jnp.mean(wide * wide, axis=-1, keepdims=True) + EPS)
    return wide * factor * gain


def cols(c):
    return slice(c * 128, c * 128 + 128)


def each(lo, hi, body):
    def step(k, carry):
        body(k)
        return carry

    lax.fori_loop(lo, hi, step, 0)


def kernel(
    x1h, x2h, sth, wqh, wkh, wvh, wddh, wduh, woh, roh, wgh, wuh, wdh,
    again, bias, dlog, wb, og, egain, ids, routes1, routes2,
    first, tail,
    x1, x2, st, wq, wk, wv, wdd, wdu, wo, ro, wg, wu, wd,
    lsem, ssem, sem,
    normed, p1, p2all, named, tp, fresh, h1s, h2s, blk, h2c, h2r,
    ax_s1, ax_s2, ax_r1, ax_r2, az_s1, az_s2, az_r1, az_r2,
    rt1, rt2, hb1, hb2, hid1, hid2,
    slots1, slots2, out1, out2, pr1, pr2, zb1, zb2, zr1, zr2,
    ex_s1, ex_s2, ex_r1, ex_r2, res1, res2,
    scr1, scr2, ez_s1, ez_s2, ez_r1, ez_r2, rows,
):
    ax_s, ax_r, az_s, az_r = (ax_s1, ax_s2), (ax_r1, ax_r2), (az_s1, az_s2), (az_r1, az_r2)
    rt, hb, hid = (rt1, rt2), (hb1, hb2), (hid1, hid2)
    slots, out, pr, zb, zr = (slots1, slots2), (out1, out2), (pr1, pr2), (zb1, zb2), (zr1, zr2)
    ex_s, ex_r, res, scr = (ex_s1, ex_s2), (ex_r1, ex_r2), (res1, res2), (scr1, scr2)
    ez_s, ez_r = (ez_s1, ez_s2), (ez_r1, ez_r2)
    dp = lax.axis_index("dp")
    ex = lax.axis_index("expert")
    y = dp // 2
    core = lax.rem(dp, 2)
    xx = ex // NZ
    z = lax.rem(ex, NZ)

    def same(s):
        return 2 * lax.rem(y + s, 4) + core

    def other(s):
        return 2 * lax.rem(y + s, 4) + 1 - core

    def xat(s):
        return lax.rem(xx + s, NX)

    def zat(s):
        return lax.rem(z + s, NZ)

    def xdev(s):
        return {"expert": xat(s) * NZ + z}

    def zdev(s):
        return {"expert": xx * NZ + zat(s)}

    def rcopy(src, dst, row, snd, rcv, device):
        return pltpu.make_async_remote_copy(
            src_ref=src,
            dst_ref=dst,
            send_sem=sem.at[row, snd],
            recv_sem=sem.at[row + 1, rcv],
            device_id=device,
            device_id_type=MESH,
        )

    loads = []
    for n, (src, dst) in enumerate(
        (
            (x2h, x2), (x1h, x1), (wqh, wq), (wkh, wk), (wvh, wv), (wddh, wdd), (wduh, wdu),
        )
    ):
        loads.append(pltpu.make_async_copy(src, dst, lsem.at[n]))

    def load_state(i):
        part = pl.ds(i * 8, 8)
        return pltpu.make_async_copy(sth.at[part], st.at[part], ssem.at[i])

    later = []
    for n, (src, dst) in enumerate(((woh, wo), (roh, ro), (wgh, wg), (wuh, wu), (wdh, wd))):
        later.append(pltpu.make_async_copy(src, dst, lsem.at[7 + n]))
    for copy in loads:
        copy.start()
    barrier = pltpu.get_barrier_semaphore()
    for s in range(1, ND):
        pl.semaphore_signal(barrier, inc=1, device_id={"dp": lax.rem(dp + s, ND)}, device_id_type=MESH)
    for s in range(1, NX):
        pl.semaphore_signal(barrier, inc=1, device_id=xdev(s), device_id_type=MESH)
    for s in range(1, NZ):
        pl.semaphore_signal(barrier, inc=1, device_id=zdev(s), device_id_type=MESH)
    each(0, 8, lambda i: load_state(i).start())
    for copy in later:
        copy.start()
    load_wo, load_ro = later[0], later[1]

    for copy in loads:
        copy.wait()
    normed[0:R1, :] = rms(x1[...].astype(F32), again[...]).astype(BF16)
    normed[R1:RT, :] = rms(x2[...].astype(F32), again[...]).astype(BF16)
    n = normed[...]

    def project(w):
        produced = dot(n, w[...])
        return produced * jax.nn.sigmoid(produced)

    def unit(v):
        return v * lax.rsqrt(jnp.sum(v * v, axis=-1, keepdims=True) + EPS)

    q = unit(project(wq))
    k = unit(project(wk))
    v = project(wv)
    low = dot(n, wdd[...]).astype(BF16)
    gate = dot(low, wdu[...]) + bias[...]
    soft = jnp.maximum(gate, 0.0) + jnp.log(1.0 + jnp.exp(-jnp.abs(gate)))
    strength = jnp.exp(jnp.full((RT, H), dlog[0], F32))
    decay = jnp.exp(-(strength * soft))
    beta = jax.nn.sigmoid(
        jnp.sum(n.astype(F32) * wb[...].astype(F32), axis=-1, keepdims=True)
    )
    dk = decay * k
    dq = decay * q
    sc = jnp.broadcast_to(beta * jnp.sum(k * q, axis=-1, keepdims=True), (RT, H))
    for c, part in enumerate((dk, dq, v, sc)):
        p2all[dp, :, cols(c)] = part[R1:RT, :].astype(BF16)
    pl.semaphore_wait(barrier, ND + NX + NZ - 3)

    def pack_copy(s, slot):
        return rcopy(
            p2all.at[dp], p2all.at[slot], PACK, s, slot, {"dp": lax.rem(dp + s, ND)}
        )

    each(1, ND, lambda s: pack_copy(s, dp).start())
    dk_hi = dk.astype(BF16).astype(F32)
    dq_hi = dq.astype(BF16).astype(F32)
    parts = (dk_hi, dk - dk_hi, dq_hi, dq - dq_hi, v, sc, decay, beta * k)
    for c, part in enumerate(parts):
        p1[:, cols(c)] = part[0:R1, :]

    m = iota((16, H), 0)

    def first_block(i):
        load_state(i).wait()
        at = pl.ds(pl.multiple_of(i * 8, 8), 8)
        t = p1[at, :]
        dcol = jnp.transpose(t[:, cols(6)])
        bcol = jnp.transpose(t[:, cols(7)])
        for j in range(8):
            row = [t[j : j + 1, cols(c)] for c in range(6)]
            state = st[i * 8 + j]
            a = jnp.where(m == 0, row[0], jnp.where(m == 1, row[1], jnp.where(m == 2, row[2], row[3])))
            got = dot(a.astype(BF16), state)
            u = row[4] - (got[0:1] + got[1:2])
            blk[j : j + 1, :] = got[2:3] + got[3:4] + row[5] * u
            fresh[i * 8 + j] = (
                state.astype(F32) * dcol[:, j : j + 1] + bcol[:, j : j + 1] * u
            ).astype(BF16)
        h1s[at, :] = rms(blk[...] * H**-0.5, og[...])

    each(0, 8, first_block)

    order = iota((R1, R1), 0)
    within = order & 15
    source = order - within + jnp.where(within < 8, 2 * within, 2 * (within - 8) + 1)
    perm = (iota((R1, R1), 1) == source).astype(BF16)

    def tile(p, val, xi, c):
        if p == 0:
            return val[xi * 16 : xi * 16 + 16, cols(c)]
        return jnp.concatenate(
            [val[xi * 8 : xi * 8 + 8, cols(2 * c)], val[xi * 8 : xi * 8 + 8, cols(2 * c + 1)]], axis=0
        )

    def a_send(p, val):
        for xi in range(NX):
            for c in range(TILES[p]):
                ax_s[p][xi, c] = tile(p, val, xi, c).astype(BF16)
        for s in (2, 1, 3):
            ax_copy(p, s, xx).start()

    def ax_copy(p, s, slot):
        return rcopy(ax_s[p].at[xat(s)], ax_r[p].at[slot], AX + KINDS * p, s, slot, xdev(s))

    def az_copy(p, s, slot):
        return rcopy(
            az_s[p].at[pl.ds(3 * zat(s), 3)], az_r[p].at[slot], AZ + KINDS * p, s, slot, zdev(s)
        )

    def az_own(p, slot):
        return rcopy(
            az_s[p].at[pl.ds(0, 3)], az_r[p].at[slot], AZ + KINDS * p, 0, slot, zdev(0)
        )

    def bz_copy(p, s, owner):
        part = hb[p].at[xx, pl.ds(3 * owner, 3)]
        return rcopy(part, part, BZ + KINDS * p, s, owner, zdev(s))

    def bx_copy(p, s, owner):
        part = hb[p].at[owner]
        return rcopy(part, part, BX + KINDS * p, s, owner, xdev(s))

    def a_turn(p):
        total = ax_s[p][xx].astype(F32)
        for s in (1, 3, 2):
            ax_copy(p, s, xat(s)).wait_recv()
            total = total + ax_r[p][xat(s)].astype(F32)
        az_s[p][...] = total.astype(BF16)
        for s in (4, 3, 5, 2, 6, 1, 7):

            @pl.when(zat(s) < OWNERS[p])
            def _():
                az_copy(p, s, z).start()

    def b_start(p):
        @pl.when(z < OWNERS[p])
        def _():
            mine = pl.ds(3 * z, 3)
            total = az_s[p][mine].astype(F32) + rt[p][xx, mine].astype(F32)
            for s in (1, 7, 2, 6, 3, 5, 4):
                az_own(p, zat(s)).wait_recv()
                total = total + az_r[p][zat(s)].astype(F32)
            hb[p][xx, mine] = total.astype(BF16)
            for s in (4, 3, 5, 2, 6, 1, 7):
                bz_copy(p, s, z).start()

    def b_turn(p):
        for s in (1, 7, 2, 6, 3, 5, 4):

            @pl.when(zat(s) < OWNERS[p])
            def _():
                bz_copy(p, s, zat(s)).wait_recv()

        for s in (2, 1, 3):
            bx_copy(p, s, xx).start()

    def b_end(p):
        for s in (1, 3, 2):
            bx_copy(p, s, xat(s)).wait_recv()
        for xi in range(NX):
            for c in range(TILES[p]):
                got = hb[p][xi, c].astype(F32)
                if p == 0:
                    hid1[xi * 16 : xi * 16 + 16, cols(c)] = got
                else:
                    hid2[xi * 8 : xi * 8 + 8, cols(2 * c)] = got[0:8]
                    hid2[xi * 8 : xi * 8 + 8, cols(2 * c + 1)] = got[8:16]

    load_wo.wait()
    a_send(0, dot(dot(perm, h1s[...].astype(BF16)).astype(BF16), wo[...]))

    base = dp * R1
    named[...] = (ids[...] == base + iota((R1, 256), 0)).astype(F32)
    for s in range(1, ND):
        pack_copy(s, lax.rem(dp + s, ND)).wait_recv()
    tp[...] = dot(named[...].astype(BF16), p2all[...].reshape(ND * R2, 4 * H))

    def second_block(i):
        at = pl.ds(pl.multiple_of(i * 8, 8), 8)
        t = tp[at, :]
        for j in range(8):
            row = [t[j : j + 1, cols(c)] for c in range(4)]
            a = jnp.where(m == 0, row[0], row[1])
            got = dot(a.astype(BF16), fresh[i * 8 + j])
            blk[j : j + 1, :] = got[1:2] + row[3] * (row[2] - got[0:1])
        h2s[at, :] = rms(blk[...] * H**-0.5, og[...])

    each(0, 8, second_block)
    h2c[...] = dot(named[...].astype(BF16), h2s[...].astype(BF16), ((0,), (0,))).astype(
        BF16
    ).reshape(ND, R2, H)

    def head_copy(s, slot):
        peer = lax.rem(dp + s, ND)
        return rcopy(h2c.at[peer], h2r.at[slot], HEAD, s, slot, {"dp": peer})

    each(1, ND, lambda s: head_copy(s, dp).start())

    xp = dot(perm, x1[...])
    x2v = x2[...].astype(F32)
    for xi in range(NX):
        for c in range(TILES[0]):
            rt1[xi, c] = tile(0, xp, xi, c).astype(BF16)
        for c in range(TILES[1]):
            rt2[xi, c] = tile(1, x2v, xi, c).astype(BF16)
    a_turn(0)

    def multi_hot(tab, count):
        hot = jnp.zeros((count, 128), F32)
        for c in range(8):
            hot = hot + (tab[:, c : c + 1] == iota((count, 128), 1)).astype(F32)
        return hot

    tab1 = routes1[pl.ds(pl.multiple_of(dp * R1, R1), R1), :]
    tab2 = routes2[pl.ds(pl.multiple_of(dp * R2, R2), R2), :]
    mask = (dot(perm, multi_hot(tab1, R1).astype(BF16)), multi_hot(tab2, R2))
    expert_a, select, place = [], [], []
    for p in range(2):
        r, n_slots, cap = ROWS[p], SLOTS[p], (3, 2)[p]
        tri = (iota((r, r), 0) >= iota((r, r), 1)).astype(BF16)
        rank = (mask[p] * dot(tri, mask[p].astype(BF16))).astype(BF16)
        sa, sb = iota((128, n_slots), 1), iota((n_slots, 128), 0)
        hot_a = iota((128, n_slots), 0) == 4 * ex + (sa >> cap)
        hot_b = iota((n_slots, 128), 1) == 4 * ex + (sb >> cap)
        at_a = (iota((r, n_slots), 1) & ((1 << cap) - 1)) + 1
        at_b = (iota((n_slots, r), 0) & ((1 << cap) - 1)) + 1
        expert_a.append(hot_a.astype(F32))
        place.append((dot(rank, hot_a.astype(BF16)) == at_a.astype(F32)).astype(F32))
        select.append((dot(hot_b.astype(BF16), rank, ((1,), (1,))) == at_b.astype(F32)).astype(BF16))

    for s in range(1, ND):
        head_copy(s, lax.rem(dp + s, ND)).wait_recv()
    h2r[dp] = h2c[dp]
    heads2 = h2r[0].astype(F32)
    for g in range(1, ND):
        heads2 = heads2 + h2r[g].astype(F32)
    a_send(1, dot(heads2.astype(BF16), wo[...]))
    b_start(0)
    a_turn(1)
    b_turn(0)
    b_start(1)

    def c_copy(p, slot, row, device):
        part = slots[p].at[slot]
        return rcopy(part, part, CC + KINDS * p, row, slot, {"dp": device})

    def c_start(p):
        normed_p = rms(hid[p][...], egain[...]).astype(BF16)
        slots[p][dp] = dot(select[p], normed_p).astype(BF16)
        for s in (2, 1, 3):
            c_copy(p, dp, s, same(s)).start()
        c_copy(p, dp, 0, other(0)).start()
        return normed_p

    def c_turn(p):
        for s in (1, 3, 2):
            c_copy(p, same(s), s, same(s)).wait_recv()
            c_copy(p, same(s), 3 + s, other(0)).start()

    def c_end(p):
        for s in (0, 1, 3, 2):
            c_copy(p, other(s), 0, other(0)).wait_recv()

    def weights(p, normed_p):
        scores = jax.nn.sigmoid(dot(normed_p, ro[...])) * mask[p]
        shares = ROUTE_SCALE * scores / jnp.sum(scores, axis=-1, keepdims=True)
        return dot(shares, expert_a[p], precision=lax.Precision.HIGHEST) * place[p]

    b_end(0)
    n0 = c_start(0)
    b_turn(1)
    load_ro.wait()
    w0 = weights(0, n0)
    b_end(1)
    n1 = c_start(1)
    w1 = weights(1, n1)
    share = (w0, w1)
    for copy in later[2:]:
        copy.wait()

    def hidden_units(x, e, mine):
        g = dot(x, wg[e])
        u = dot(x, wu[e])
        return jnp.where(mine, g * jax.nn.sigmoid(g) * u, 0.0).astype(BF16)

    spot = iota((ND * 16, H), 0) & 15

    def experts(p):
        if p == 0:
            for pair in range(2):
                x = slots1[:, 16 * pair : 16 * pair + 16, :].reshape(ND * 16, D)
                a0 = hidden_units(x, 2 * pair, (spot >> 3) == 0)
                a1 = hidden_units(x, 2 * pair + 1, (spot >> 3) == 1)
                for c in range(0, D, 768):
                    cc = slice(c, c + 768)
                    got = dot(a0, wd[2 * pair, :, cc]) + dot(a1, wd[2 * pair + 1, :, cc])
                    out1[:, 16 * pair : 16 * pair + 16, cc] = got.astype(BF16).reshape(ND, 16, 768)
        else:
            x = slots2[...].reshape(ND * 16, D)
            acts = [hidden_units(x, e, (spot >> 2) == e) for e in range(4)]
            for c in range(0, D, 768):
                cc = slice(c, c + 768)
                got = dot(acts[0], wd[0, :, cc])
                for e in range(1, 4):
                    got = got + dot(acts[e], wd[e, :, cc])
                out2[:, :, cc] = got.astype(BF16).reshape(ND, 16, 768)

    def pair_copy(p, s):
        yy = lax.rem(y + s, 4)
        return rcopy(out[p].at[other(s)], pr[p].at[yy], DP + KINDS * p, yy, yy, {"dp": other(0)})

    def chip_copy(p, s, slot):
        yy = lax.rem(y + s, 4)
        return rcopy(zb[p].at[yy], zr[p].at[slot], DY + KINDS * p, yy, slot, {"dp": same(s)})

    def d_start(p):
        for s in (2, 1, 3, 0):
            pair_copy(p, s).start()

    def d_turn(p):
        for s in (2, 1, 3):
            yy = lax.rem(y + s, 4)
            pair_copy(p, s).wait_recv()
            zb[p][yy] = (out[p][same(s)].astype(F32) + pr[p][yy].astype(F32)).astype(BF16)
            chip_copy(p, s, y).start()
        pair_copy(p, 0).wait_recv()

    def ex_copy(p, s, slot):
        return rcopy(ex_s[p].at[xat(s)], ex_r[p].at[slot], EX + KINDS * p, s, slot, xdev(s))

    def ez_copy(p, s, slot):
        return rcopy(ez_s[p].at[zat(s)], ez_r[p].at[slot], EZ + KINDS * p, s, slot, zdev(s))

    def e_start(p):
        total = out[p][dp].astype(F32) + pr[p][y].astype(F32)
        for s in (1, 3, 2):
            yy = lax.rem(y + s, 4)
            chip_copy(p, s, yy).wait_recv()
            total = total + zr[p][yy].astype(F32)
        summed = total.astype(BF16)
        w_hi = share[p].astype(BF16)
        w_lo = (share[p] - w_hi.astype(F32)).astype(BF16)
        got = dot(w_hi, summed) + dot(w_lo, summed)
        res[p][...] = got
        for xi in range(NX):
            for c in range(TILES[p]):
                ex_s[p][xi, c] = tile(p, got, xi, c).astype(BF16)
        for s in (2, 1, 3):
            ex_copy(p, s, xx).start()

    def e_turn(p):
        block = (16, 8)[p]
        at = pl.ds(pl.multiple_of(xx * block, block), block)
        own = (iota((block, 128), 0) & 7) == z
        for s in (1, 3, 2):
            ex_copy(p, s, xat(s)).wait_recv()
        scr[p][...] = jnp.zeros_like(scr[p])
        for c in range(TILES[p]):
            arrived = ex_r[p][xat(1), c].astype(F32)
            for s in (2, 3):
                arrived = arrived + ex_r[p][xat(s), c].astype(F32)
            for half in range(2):
                ct = c if p == 0 else 2 * c + half
                if p == 0 and half == 1:
                    continue
                mine = res[p][at, cols(ct)] + jnp.where(own, hid[p][at, cols(ct)], 0.0)
                if p == 0:
                    val = mine + arrived
                    scr1[pl.ds(ct, NZ, stride=48), :] = val[0:8]
                    scr1[pl.ds(NCT + ct, NZ, stride=48), :] = val[8:16]
                else:
                    scr2[pl.ds(ct, NZ, stride=32), :] = mine + arrived[8 * half : 8 * half + 8]
        w = OUTS[p]
        for zi in range(NZ):
            ez_s[p][zi] = scr[p][zi * w : zi * w + w, :].astype(BF16)
        for s in (4, 3, 5, 2, 6, 1, 7):
            ez_copy(p, s, z).start()

    def e_end(p):
        w = OUTS[p]
        total = scr[p][pl.ds(pl.multiple_of(z * w, w), w), :]
        for s in (1, 7, 2, 6, 3, 5, 4):
            ez_copy(p, s, zat(s)).wait_recv()
            total = total + ez_r[p][zat(s)].astype(F32)
        for j in range(2 - p):
            for ct in range(NCT):
                rows[2 * p + j : 2 * p + j + 1, cols(ct)] = total[j * NCT + ct : j * NCT + ct + 1, :]

    c_turn(0)
    c_end(0)
    experts(0)
    d_start(0)
    c_turn(1)
    d_turn(0)
    c_end(1)
    experts(1)
    d_start(1)
    d_turn(1)
    e_start(0)
    e_start(1)
    e_turn(0)
    e_turn(1)
    e_end(0)
    e_end(1)
    first[...] = rows[0:2, :].astype(BF16)
    tail[...] = rows[2:3, :].astype(BF16)

    each(1, ND, lambda s: pack_copy(s, dp).wait_send())
    each(1, ND, lambda s: head_copy(s, dp).wait_send())
    for p in range(2):
        for s in range(1, NX):
            ax_copy(p, s, xx).wait_send()
            bx_copy(p, s, xx).wait_send()
            ex_copy(p, s, xx).wait_send()
            chip_copy(p, s, y).wait_send()
            c_copy(p, dp, s, same(s)).wait_send()
            c_copy(p, same(s), 3 + s, other(0)).wait_send()
        for s in range(4):
            pair_copy(p, s).wait_send()
        c_copy(p, dp, 0, other(0)).wait_send()
        for s in range(1, NZ):
            ez_copy(p, s, z).wait_send()

            @pl.when(zat(s) < OWNERS[p])
            def _():
                az_copy(p, s, z).wait_send()

        @pl.when(z < OWNERS[p])
        def _():
            for s in range(1, NZ):
                bz_copy(p, s, z).wait_send()


VM = pl.BlockSpec(memory_space=pltpu.VMEM)
SM = pl.BlockSpec(memory_space=pltpu.SMEM)
HB = pl.BlockSpec(memory_space=pl.ANY)
DMA = pltpu.SemaphoreType.DMA


def on_device(
    inputs, tail_inputs, states, tail_ids, routes, tail_routes, attention_gain,
    query_weight, key_weight, value_weight, decay_down, decay_up, decay_bias,
    decay_log, beta_weight, output_gain, head_out, expert_gain, router_weight,
    gate_weight, up_weight, down_weight,
):
    def vm(*dims, dtype=BF16):
        return pltpu.VMEM(dims, dtype)

    def both(lead, rest, sizes, dtype=BF16):
        return [vm(*lead, n, *rest, dtype=dtype) for n in sizes]

    heavy = (
        inputs, tail_inputs, states.reshape(R1, H, H), query_weight, key_weight,
        value_weight, decay_down, decay_up, head_out, router_weight, gate_weight,
        up_weight, down_weight,
    )
    scratch = [vm(*a.shape) for a in heavy]
    scratch += [DMA((12,)), DMA((8,)), DMA((SEM_ROWS, 8))]
    scratch += [
        vm(RT, D), vm(R1, 8 * H, dtype=F32), vm(ND, R2, 4 * H), vm(R1, 256, dtype=F32),
        vm(R1, 4 * H, dtype=F32), vm(R1, H, H), vm(R1, H, dtype=F32), vm(R1, H, dtype=F32),
        vm(8, H, dtype=F32), vm(ND, R2, H), vm(ND, R2, H),
    ]
    t = (16, 128)
    scratch += both((NX,), t, TILES) + both((NX,), t, TILES)
    scratch += both((), t, TILES) + [vm(NZ, 3, *t), vm(NZ, 3, *t)]
    scratch += both((NX,), t, TILES) + both((NX,), t, TILES)
    scratch += both((), (D,), ROWS, F32)
    scratch += both((ND,), (D,), SLOTS) + both((ND,), (D,), SLOTS)
    scratch += both((4,), (D,), SLOTS) + both((4,), (D,), SLOTS) + both((4,), (D,), SLOTS)
    scratch += both((NX,), t, TILES) + both((NX,), t, TILES)
    scratch += both((), (D,), ROWS, F32)
    scratch += [vm(NZ * w, 128, dtype=F32) for w in OUTS]
    scratch += both((NZ,), (128,), OUTS) + both((NZ,), (128,), OUTS)
    scratch += [vm(8, D, dtype=F32)]
    return pl.pallas_call(
        kernel,
        out_shape=(jax.ShapeDtypeStruct((2, D), BF16), jax.ShapeDtypeStruct((1, D), BF16)),
        in_specs=[HB] * 13 + [VM, VM, SM] + [VM] * 6,
        out_specs=(VM, VM),
        scratch_shapes=scratch,
        compiler_params=pltpu.CompilerParams(
            vmem_limit_bytes=VMEM_LIMIT, collective_id=0, has_side_effects=True
        ),
        name="two_steps",
    )(
        *heavy,
        attention_gain.reshape(1, D), decay_bias.reshape(1, H), decay_log,
        beta_weight.reshape(1, D), output_gain.reshape(1, H), expert_gain.reshape(1, D),
        tail_ids.reshape(1, 256), routes, tail_routes,
    )


def solution(mesh):
    placed = (
        P("dp", None),
        P("dp", None),
        P("dp", "expert", None, None),
        P(),
        P(),
        P(),
        P(),
        P(None, "expert"),
        P(None, "expert"),
        P(None, "expert"),
        P(),
        P(None, "expert"),
        P("expert"),
        P("expert"),
        P(None, "expert"),
        P(),
        P("expert", None),
        P(),
        P(),
        P("expert", None, "dp"),
        P("expert", None, "dp"),
        P("expert", "dp", None),
    )
    return jax.shard_map(
        on_device,
        mesh=mesh,
        in_specs=placed,
        out_specs=(P(("dp", "expert"), None), P(("dp", "expert"), None)),
        check_vma=False,
    )
```

time: 490 us -> 81.6 us (0.17)
  waiting for transfers between devices: 321 us -> 0 us
  Pallas kernels: 0 us -> 70.6 us
  matrix products: 54 us -> 0 us
  local copies, waits for them, and re-layouts: 43.3 us -> 8.26 us
  other arithmetic: 24.7 us -> 0 us
  blocking collectives: 18.7 us -> 0 us
  between operations: 15.9 us -> 1.29 us
  starting transfers between devices: 7.98 us -> 0 us
    unnamed x6 -> x0, waiting for transfers between devices: 145 us -> none
    psum x1 -> x0, waiting for transfers between devices: 142 us -> none  [attend(): lax.psum(partial_value.astype(jnp.bfloat16), 'expert').astype(jnp.float32)]
    pallas_call x0 -> x1, Pallas kernels: none -> 70.6 us  [on_device(): pl.pallas_call(kernel, out_shape=(jax.ShapeDtypeStruct((2, D), BF16), jax...]
    dot_general x27 -> x0, matrix products: 54 us -> none  [the longest x6 9.42 us: project(): produced = jnp.dot(normed, weight, preferred_element_type=jnp.float32)]
    reduce_scatter x2 -> x0, waiting for transfers between devices: 34.3 us -> none  [mixture(): lax.psum_scatter(results.reshape(per_group * lax.axis_size('dp'), feature...]
    gather x10 -> x0, local copies, waits for them, and re-layouts: 34.2 us -> none  [the longest x6 24.1 us: slot_weights(): chosen = jnp.take_along_axis(scores, slot_routes, axis=-1)]
    all_gather x1 -> x0, blocking collectives: 18.7 us -> none  [mixture(): gathered = lax.all_gather(sent_rows, 'dp', axis=0, tiled=True)]
    all_to_all x1 -> x0, starting transfers between devices: 7.59 us -> none  [migrate(): lax.all_to_all(picked, 'dp', split_axis=0, concat_axis=0, tiled=True)]
  transfers between devices with their start and end apart: 6 -> 0, of which waited for: 4 -> 0; matrix products, arithmetic and copies ran while one was open for 16% -> 0% of each run, Pallas kernels for 0% -> 0%
where the time goes in v2:
time: 81.6 us; the launch traced here: 80.1 us
  Pallas kernels  70.6 us (87%)
  local copies, waits for them, and re-layouts  8.26 us (10%)
  between operations  1.29 us (2%)
    pallas_call x1, Pallas kernels, on_device(): pl.pallas_call(kernel, out_shape=(jax.ShapeDtypeStruct((2, D), BF16), jax...  70.6 us
    unnamed x4, local copies, waits for them, and re-layouts  5.64 us

profile of v2, /device:TPU:1, one launch (start us, length us, event | category | flops | bytes accessed | tf_op | source)
XLA Modules:
  0.0 80.1 jit_solution(15164145719012770351)
XLA Ops:
  1.3 1.3 %reshape.26.again = f32[1,2304]{1,0:T(1,128)} reshape(f32[2304]{0:T(1024)} %param.28) | data formatting | bytes 18432 | tf_op jit(solution)/shard_map/reshape | solution.py:613
  2.6 1.3 %reshape.30.egain = f32[1,2304]{1,0:T(1,128)} reshape(f32[2304]{0:T(1024)} %param.39) | data formatting | bytes 18432 | tf_op jit(solution)/shard_map/reshape | solution.py:614
  3.9 1.5 %copy.25.routes2 = s32[256,8]{1,0:T(8,128)} copy(s32[256,8]{0,1:T(8,128)} %param.27) | data formatting | bytes 16384 | tf_op args[5]
  5.4 1.5 %copy.24.routes1 = s32[512,8]{1,0:T(8,128)} copy(s32[512,8]{0,1:T(8,128)} %param.26) | data formatting | bytes 32768 | tf_op args[4]
  6.9 70.6 %two_steps.1 = (bf16[2,2304]{1,0:T(2,128)(2,1)}, bf16[1,2304]{1,0:T(2,128)(2,1)}) custom-call(bf16[64,2304]{1,0:T(8,128)(2,1)} %x1h.1, bf16[32,2304]{1,0:T(8,128)(2,1)} %x2h.1, bf16[64,128,128]{2,1,0:T(8,128)(2,1)} %bitcast.5, bf16[2304,128]{1,0:T(8,128)(2,1)} %wqh.1, bf16[2304,128]{1,0:T(8,128)(2,1)} %wkh.1, bf16[2304,128]{1,0:T(8,128)(2,1)} %wvh.1, ...), custom_call_target="tpu_custom_call" | custom-call | tf_op jit(solution)/shard_map/two_steps/pallas_call | solution.py:601
  77.5 1.3 %copy.29 = bf16[2,2304]{1,0:T(2,128)(2,1)} copy(bf16[2,2304]{1,0:T(2,128)(2,1)} %get-tuple-element.4) | data formatting | bytes 18432
  78.8 1.3 %copy.30 = bf16[1,2304]{1,0:T(2,128)(2,1)} copy(bf16[1,2304]{1,0:T(2,128)(2,1)} %get-tuple-element.5) | data formatting | bytes 9216

commit v3 on v2

--- a/solution.py
+++ b/solution.py
@@ -1,3 +1,5 @@
+import functools
+
 import jax
 import jax.numpy as jnp
 from jax import lax
@@ -61,8 +63,8 @@
 def kernel(
     x1h, x2h, sth, wqh, wkh, wvh, wddh, wduh, woh, roh, wgh, wuh, wdh,
     again, bias, dlog, wb, og, egain, ids, routes1, routes2,
-    first, tail,
-    x1, x2, st, wq, wk, wv, wdd, wdu, wo, ro, wg, wu, wd,
+    final,
+    x1, x2, st, wall, wdu, wo, ro, wgu, wd,
     lsem, ssem, sem,
     normed, p1, p2all, named, tp, fresh, h1s, h2s, blk, h2c, h2r,
     ax_s1, ax_s2, ax_r1, ax_r2, az_s1, az_s2, az_r1, az_r2,
@@ -111,10 +113,22 @@
             device_id_type=MESH,
         )
 
+    sent = []
+
+    def send(make):
+        make().start()
+        sent.append(lambda: make().wait_send())
+
+    def send_if(where, make):
+        pl.when(where)(lambda: make().start())
+        sent.append(lambda: pl.when(where)(lambda: make().wait_send()))
+
     loads = []
     for n, (src, dst) in enumerate(
         (
-            (x2h, x2), (x1h, x1), (wqh, wq), (wkh, wk), (wvh, wv), (wddh, wdd), (wduh, wdu),
+            (x2h, x2), (x1h, x1), (wqh, wall.at[:, pl.ds(0, H)]),
+            (wkh, wall.at[:, pl.ds(H, H)]), (wvh, wall.at[:, pl.ds(2 * H, H)]),
+            (wddh, wall.at[:, pl.ds(3 * H, H)]), (wduh, wdu),
         )
     ):
         loads.append(pltpu.make_async_copy(src, dst, lsem.at[n]))
@@ -124,7 +138,7 @@
         return pltpu.make_async_copy(sth.at[part], st.at[part], ssem.at[i])
 
     later = []
-    for n, (src, dst) in enumerate(((woh, wo), (roh, ro), (wgh, wg), (wuh, wu), (wdh, wd))):
+    for n, (src, dst) in enumerate(((woh, wo), (roh, ro), (wgh, wgu.at[:, :, pl.ds(0, H)]), (wuh, wgu.at[:, :, pl.ds(H, H)]), (wdh, wd))):
         later.append(pltpu.make_async_copy(src, dst, lsem.at[7 + n]))
     for copy in loads:
         copy.start()
@@ -135,28 +149,38 @@
         pl.semaphore_signal(barrier, inc=1, device_id=xdev(s), device_id_type=MESH)
     for s in range(1, NZ):
         pl.semaphore_signal(barrier, inc=1, device_id=zdev(s), device_id_type=MESH)
-    each(0, 8, lambda i: load_state(i).start())
-    for copy in later:
-        copy.start()
+
+    def load_block(k):
+        block = xat(k + 1)
+        load_state(2 * block).start()
+        load_state(2 * block + 1).start()
+
+    each(0, NX, load_block)
+    later[0].start()
     load_wo, load_ro = later[0], later[1]
 
+    again_row = again[...].reshape(1, D)
+    egain_row = egain[...].reshape(1, D)
     for copy in loads:
         copy.wait()
-    normed[0:R1, :] = rms(x1[...].astype(F32), again[...]).astype(BF16)
-    normed[R1:RT, :] = rms(x2[...].astype(F32), again[...]).astype(BF16)
+    for copy in later[1:]:
+        copy.start()
+    normed[0:R1, :] = rms(x1[...].astype(F32), again_row).astype(BF16)
+    normed[R1:RT, :] = rms(x2[...].astype(F32), again_row).astype(BF16)
     n = normed[...]
-
-    def project(w):
-        produced = dot(n, w[...])
+    every = dot(n, wall[...])
+
+    def project(c):
+        produced = every[:, cols(c)]
         return produced * jax.nn.sigmoid(produced)
 
     def unit(v):
         return v * lax.rsqrt(jnp.sum(v * v, axis=-1, keepdims=True) + EPS)
 
-    q = unit(project(wq))
-    k = unit(project(wk))
-    v = project(wv)
-    low = dot(n, wdd[...]).astype(BF16)
+    q = unit(project(0))
+    k = unit(project(1))
+    v = project(2)
+    low = every[:, cols(3)].astype(BF16)
     gate = dot(low, wdu[...]) + bias[...]
     soft = jnp.maximum(gate, 0.0) + jnp.log(1.0 + jnp.exp(-jnp.abs(gate)))
     strength = jnp.exp(jnp.full((RT, H), dlog[0], F32))
@@ -177,6 +201,7 @@
         )
 
     each(1, ND, lambda s: pack_copy(s, dp).start())
+    sent.append(lambda: each(1, ND, lambda s: pack_copy(s, dp).wait_send()))
     dk_hi = dk.astype(BF16).astype(F32)
     dq_hi = dq.astype(BF16).astype(F32)
     parts = (dk_hi, dk - dk_hi, dq_hi, dq - dq_hi, v, sc, decay, beta * k)
@@ -203,12 +228,11 @@
             ).astype(BF16)
         h1s[at, :] = rms(blk[...] * H**-0.5, og[...])
 
-    each(0, 8, first_block)
-
     order = iota((R1, R1), 0)
     within = order & 15
     source = order - within + jnp.where(within < 8, 2 * within, 2 * (within - 8) + 1)
     perm = (iota((R1, R1), 1) == source).astype(BF16)
+    perm16 = perm[0:16, 0:16]
 
     def tile(p, val, xi, c):
         if p == 0:
@@ -222,7 +246,7 @@
             for c in range(TILES[p]):
                 ax_s[p][xi, c] = tile(p, val, xi, c).astype(BF16)
         for s in (2, 1, 3):
-            ax_copy(p, s, xx).start()
+            send(functools.partial(ax_copy, p, s, xx))
 
     def ax_copy(p, s, slot):
         return rcopy(ax_s[p].at[xat(s)], ax_r[p].at[slot], AX + KINDS * p, s, slot, xdev(s))
@@ -247,15 +271,12 @@
 
     def a_turn(p):
         total = ax_s[p][xx].astype(F32)
-        for s in (1, 3, 2):
+        for s in (3, 2, 1):
             ax_copy(p, s, xat(s)).wait_recv()
             total = total + ax_r[p][xat(s)].astype(F32)
         az_s[p][...] = total.astype(BF16)
         for s in (4, 3, 5, 2, 6, 1, 7):
-
-            @pl.when(zat(s) < OWNERS[p])
-            def _():
-                az_copy(p, s, z).start()
+            send_if(zat(s) < OWNERS[p], functools.partial(az_copy, p, s, z))
 
     def b_start(p):
         @pl.when(z < OWNERS[p])
@@ -269,6 +290,12 @@
             for s in (4, 3, 5, 2, 6, 1, 7):
                 bz_copy(p, s, z).start()
 
+        def left():
+            for s in range(1, NZ):
+                bz_copy(p, s, z).wait_send()
+
+        sent.append(lambda: pl.when(z < OWNERS[p])(left))
+
     def b_turn(p):
         for s in (1, 7, 2, 6, 3, 5, 4):
 
@@ -277,7 +304,7 @@
                 bz_copy(p, s, zat(s)).wait_recv()
 
         for s in (2, 1, 3):
-            bx_copy(p, s, xx).start()
+            send(functools.partial(bx_copy, p, s, xx))
 
     def b_end(p):
         for s in (1, 3, 2):
@@ -292,7 +319,22 @@
                     hid2[xi * 8 : xi * 8 + 8, cols(2 * c + 1)] = got[8:16]
 
     load_wo.wait()
-    a_send(0, dot(dot(perm, h1s[...].astype(BF16)).astype(BF16), wo[...]))
+
+    def first_x(k):
+        s = lax.rem(k + 1, NX)
+        xi = xat(s)
+        each(0, 2, lambda b: first_block(2 * xi + b))
+        h16 = h1s[pl.ds(pl.multiple_of(xi * 16, 16), 16), :].astype(BF16)
+        val = dot(dot(perm16, h16).astype(BF16), wo[...])
+        for c in range(NCT):
+            ax_s1[xi, c] = val[:, cols(c)].astype(BF16)
+
+        @pl.when(k < NX - 1)
+        def _():
+            ax_copy(0, s, xx).start()
+
+    each(0, NX, first_x)
+    sent.append(lambda: each(1, NX, lambda s: ax_copy(0, s, xx).wait_send()))
 
     base = dp * R1
     named[...] = (ids[...] == base + iota((R1, 256), 0)).astype(F32)
@@ -320,6 +362,7 @@
         return rcopy(h2c.at[peer], h2r.at[slot], HEAD, s, slot, {"dp": peer})
 
     each(1, ND, lambda s: head_copy(s, dp).start())
+    sent.append(lambda: each(1, ND, lambda s: head_copy(s, dp).wait_send()))
 
     xp = dot(perm, x1[...])
     x2v = x2[...].astype(F32)
@@ -333,11 +376,19 @@
     def multi_hot(tab, count):
         hot = jnp.zeros((count, 128), F32)
         for c in range(8):
-            hot = hot + (tab[:, c : c + 1] == iota((count, 128), 1)).astype(F32)
+            hot = hot + (tab[:, c : c + 1] == iota((count, 128), 1).astype(F32)).astype(F32)
         return hot
 
-    tab1 = routes1[pl.ds(pl.multiple_of(dp * R1, R1), R1), :]
-    tab2 = routes2[pl.ds(pl.multiple_of(dp * R2, R2), R2), :]
+    def own_table(table, count):
+        per = 128 // count
+        lanes = pl.ds(pl.multiple_of(dp // per * 128, 128), 128)
+        turned = jnp.transpose(table[:, lanes].astype(F32))
+        got = turned[0:count]
+        for g in range(1, per):
+            got = jnp.where(lax.rem(dp, per) == g, turned[g * count : g * count + count], got)
+        return got
+
+    tab1, tab2 = own_table(routes1, R1), own_table(routes2, R2)
     mask = (dot(perm, multi_hot(tab1, R1).astype(BF16)), multi_hot(tab2, R2))
     expert_a, select, place = [], [], []
     for p in range(2):
@@ -370,17 +421,17 @@
         return rcopy(part, part, CC + KINDS * p, row, slot, {"dp": device})
 
     def c_start(p):
-        normed_p = rms(hid[p][...], egain[...]).astype(BF16)
+        normed_p = rms(hid[p][...], egain_row).astype(BF16)
         slots[p][dp] = dot(select[p], normed_p).astype(BF16)
         for s in (2, 1, 3):
-            c_copy(p, dp, s, same(s)).start()
-        c_copy(p, dp, 0, other(0)).start()
+            send(functools.partial(c_copy, p, dp, s, same(s)))
+        send(functools.partial(c_copy, p, dp, 0, other(0)))
         return normed_p
 
     def c_turn(p):
         for s in (1, 3, 2):
             c_copy(p, same(s), s, same(s)).wait_recv()
-            c_copy(p, same(s), 3 + s, other(0)).start()
+            send(functools.partial(c_copy, p, same(s), 3 + s, other(0)))
 
     def c_end(p):
         for s in (0, 1, 3, 2):
@@ -404,8 +455,8 @@
         copy.wait()
 
     def hidden_units(x, e, mine):
-        g = dot(x, wg[e])
-        u = dot(x, wu[e])
+        both = dot(x, wgu[e])
+        g, u = both[:, 0:H], both[:, H : 2 * H]
         return jnp.where(mine, g * jax.nn.sigmoid(g) * u, 0.0).astype(BF16)
 
     spot = iota((ND * 16, H), 0) & 15
@@ -440,14 +491,14 @@
 
     def d_start(p):
         for s in (2, 1, 3, 0):
-            pair_copy(p, s).start()
+            send(functools.partial(pair_copy, p, s))
 
     def d_turn(p):
         for s in (2, 1, 3):
             yy = lax.rem(y + s, 4)
             pair_copy(p, s).wait_recv()
             zb[p][yy] = (out[p][same(s)].astype(F32) + pr[p][yy].astype(F32)).astype(BF16)
-            chip_copy(p, s, y).start()
+            send(functools.partial(chip_copy, p, s, y))
         pair_copy(p, 0).wait_recv()
 
     def ex_copy(p, s, slot):
@@ -471,7 +522,7 @@
             for c in range(TILES[p]):
                 ex_s[p][xi, c] = tile(p, got, xi, c).astype(BF16)
         for s in (2, 1, 3):
-            ex_copy(p, s, xx).start()
+            send(functools.partial(ex_copy, p, s, xx))
 
     def e_turn(p):
         block = (16, 8)[p]
@@ -499,7 +550,7 @@
         for zi in range(NZ):
             ez_s[p][zi] = scr[p][zi * w : zi * w + w, :].astype(BF16)
         for s in (4, 3, 5, 2, 6, 1, 7):
-            ez_copy(p, s, z).start()
+            send(functools.partial(ez_copy, p, s, z))
 
     def e_end(p):
         w = OUTS[p]
@@ -527,33 +578,15 @@
     e_turn(1)
     e_end(0)
     e_end(1)
-    first[...] = rows[0:2, :].astype(BF16)
-    tail[...] = rows[2:3, :].astype(BF16)
-
-    each(1, ND, lambda s: pack_copy(s, dp).wait_send())
-    each(1, ND, lambda s: head_copy(s, dp).wait_send())
-    for p in range(2):
-        for s in range(1, NX):
-            ax_copy(p, s, xx).wait_send()
-            bx_copy(p, s, xx).wait_send()
-            ex_copy(p, s, xx).wait_send()
-            chip_copy(p, s, y).wait_send()
-            c_copy(p, dp, s, same(s)).wait_send()
-            c_copy(p, same(s), 3 + s, other(0)).wait_send()
-        for s in range(4):
-            pair_copy(p, s).wait_send()
-        c_copy(p, dp, 0, other(0)).wait_send()
-        for s in range(1, NZ):
-            ez_copy(p, s, z).wait_send()
-
-            @pl.when(zat(s) < OWNERS[p])
-            def _():
-                az_copy(p, s, z).wait_send()
-
-        @pl.when(z < OWNERS[p])
-        def _():
-            for s in range(1, NZ):
-                bz_copy(p, s, z).wait_send()
+    final[...] = rows[...]
+
+    for left in sent:
+        left()
+
+
+def write_kernel(final, first, tail):
+    first[...] = final[0:2, :].astype(BF16)
+    tail[...] = final[2:3, :].astype(BF16)
 
 
 VM = pl.BlockSpec(memory_space=pltpu.VMEM)
@@ -579,7 +612,10 @@
         value_weight, decay_down, decay_up, head_out, router_weight, gate_weight,
         up_weight, down_weight,
     )
-    scratch = [vm(*a.shape) for a in heavy]
+    scratch = [
+        vm(R1, D), vm(R2, D), vm(R1, H, H), vm(D, 4 * H), vm(H, H), vm(H, D), vm(D, 128),
+        vm(4, D, 2 * H), vm(4, H, D),
+    ]
     scratch += [DMA((12,)), DMA((8,)), DMA((SEM_ROWS, 8))]
     scratch += [
         vm(RT, D), vm(R1, 8 * H, dtype=F32), vm(ND, R2, 4 * H), vm(R1, 256, dtype=F32),
@@ -598,11 +634,11 @@
     scratch += [vm(NZ * w, 128, dtype=F32) for w in OUTS]
     scratch += both((NZ,), (128,), OUTS) + both((NZ,), (128,), OUTS)
     scratch += [vm(8, D, dtype=F32)]
-    return pl.pallas_call(
+    final = pl.pallas_call(
         kernel,
-        out_shape=(jax.ShapeDtypeStruct((2, D), BF16), jax.ShapeDtypeStruct((1, D), BF16)),
+        out_shape=jax.ShapeDtypeStruct((8, D), F32),
         in_specs=[HB] * 13 + [VM, VM, SM] + [VM] * 6,
-        out_specs=(VM, VM),
+        out_specs=VM,
         scratch_shapes=scratch,
         compiler_params=pltpu.CompilerParams(
             vmem_limit_bytes=VMEM_LIMIT, collective_id=0, has_side_effects=True
@@ -610,10 +646,17 @@
         name="two_steps",
     )(
         *heavy,
-        attention_gain.reshape(1, D), decay_bias.reshape(1, H), decay_log,
-        beta_weight.reshape(1, D), output_gain.reshape(1, H), expert_gain.reshape(1, D),
-        tail_ids.reshape(1, 256), routes, tail_routes,
+        attention_gain, decay_bias.reshape(1, H), decay_log,
+        beta_weight.reshape(1, D), output_gain.reshape(1, H), expert_gain,
+        tail_ids.reshape(1, 256), routes.T, tail_routes.T,
     )
+    return pl.pallas_call(
+        write_kernel,
+        out_shape=(jax.ShapeDtypeStruct((2, D), BF16), jax.ShapeDtypeStruct((1, D), BF16)),
+        in_specs=[VM],
+        out_specs=(VM, VM),
+        name="write",
+    )(final)
 
 
 def solution(mesh):

time: 81.6 us -> 72.7 us (0.89); the launches traced: 80.1 us -> 72.5 us
  local copies, waits for them, and re-layouts: 8.26 us -> 0 us
    unnamed x4 -> x0, local copies, waits for them, and re-layouts: 5.64 us -> none
    reshape x2 -> x0, local copies, waits for them, and re-layouts: 2.62 us -> none  [the longest x1 1.31 us: on_device(): attention_gain.reshape(1, D)]
    pallas_call x1 -> x2, Pallas kernels: 70.6 us -> 71.2 us  [the longest x1 69.7 us: on_device(): pl.pallas_call(kernel, out_shape=jax.ShapeDtypeStruct((8, D), F32), in_sp...]
where the time goes in v3:
time: 72.7 us; the launch traced here: 72.5 us
  Pallas kernels  71.2 us (98%)
  between operations  1.29 us (2%)
    pallas_call x1, Pallas kernels, on_device(): pl.pallas_call(kernel, out_shape=jax.ShapeDtypeStruct((8, D), F32), in_sp...  69.7 us
    pallas_call x1, Pallas kernels, on_device(): pl.pallas_call(write_kernel, out_shape=(jax.ShapeDtypeStruct((2, D), BF16...  1.5 us

profile of v3, /device:TPU:1, one launch (start us, length us, event | category | flops | bytes accessed | tf_op | source)
XLA Modules:
  0.0 72.5 jit_solution(1672265496868672720)
XLA Ops:
  1.3 69.7 %two_steps.1.final = f32[8,2304]{1,0:T(8,128)} custom-call(bf16[64,2304]{1,0:T(8,128)(2,1)} %x1h.1, bf16[32,2304]{1,0:T(8,128)(2,1)} %x2h.1, bf16[64,128,128]{2,1,0:T(8,128)(2,1)} %bitcast.7, bf16[2304,128]{1,0:T(8,128)(2,1)} %wqh.1, bf16[2304,128]{1,0:T(8,128)(2,1)} %wkh.1, bf16[2304,128]{1,0:T(8,128)(2,1)} %wvh.1, bf16[2304,128]{1,0:T(8,128)(2,1)} %wddh.1, ...), custom_call_target="tpu_custom_call" | custom-call | tf_op jit(solution)/shard_map/two_steps/pallas_call | solution.py:637
  71.0 1.5 %write.1 = (bf16[2,2304]{1,0:T(2,128)(2,1)}, bf16[1,2304]{1,0:T(2,128)(2,1)}) custom-call(f32[8,2304]{1,0:T(8,128)} %two_steps.1.final), custom_call_target="tpu_custom_call" | custom-call | tf_op jit(solution)/shard_map/write/pallas_call | solution.py:653

commit v4 on v3

--- a/solution.py
+++ b/solution.py
@@ -18,6 +18,7 @@
 NCT = D // 128
 R1 = 64
 R2 = 32
+SECOND = 16
 RT = R1 + R2
 ND = 8
 NX = 4
@@ -66,7 +67,7 @@
     final,
     x1, x2, st, wall, wdu, wo, ro, wgu, wd,
     lsem, ssem, sem,
-    normed, p1, p2all, named, tp, fresh, h1s, h2s, blk, h2c, h2r,
+    normed, p1, p2all, w2, named, tp, fresh, h2s, h2c, h2r,
     ax_s1, ax_s2, ax_r1, ax_r2, az_s1, az_s2, az_r1, az_r2,
     rt1, rt2, hb1, hb2, hid1, hid2,
     slots1, slots2, out1, out2, pr1, pr2, zb1, zb2, zr1, zr2,
@@ -191,8 +192,8 @@
     dk = decay * k
     dq = decay * q
     sc = jnp.broadcast_to(beta * jnp.sum(k * q, axis=-1, keepdims=True), (RT, H))
-    for c, part in enumerate((dk, dq, v, sc)):
-        p2all[dp, :, cols(c)] = part[R1:RT, :].astype(BF16)
+    p2all[dp] = (dq - sc * dk)[R1:RT, :].astype(BF16)
+    w2[...] = (sc * v)[R1:RT, :]
     pl.semaphore_wait(barrier, ND + NX + NZ - 3)
 
     def pack_copy(s, slot):
@@ -210,23 +211,22 @@
 
     m = iota((16, H), 0)
 
-    def first_block(i):
-        load_state(i).wait()
-        at = pl.ds(pl.multiple_of(i * 8, 8), 8)
-        t = p1[at, :]
+    def first_rows(start, count):
+        t = p1[pl.ds(pl.multiple_of(start, count), count), :]
         dcol = jnp.transpose(t[:, cols(6)])
         bcol = jnp.transpose(t[:, cols(7)])
-        for j in range(8):
+        reads = []
+        for j in range(count):
             row = [t[j : j + 1, cols(c)] for c in range(6)]
-            state = st[i * 8 + j]
+            state = st[start + j]
             a = jnp.where(m == 0, row[0], jnp.where(m == 1, row[1], jnp.where(m == 2, row[2], row[3])))
             got = dot(a.astype(BF16), state)
             u = row[4] - (got[0:1] + got[1:2])
-            blk[j : j + 1, :] = got[2:3] + got[3:4] + row[5] * u
-            fresh[i * 8 + j] = (
+            reads.append(got[2:3] + got[3:4] + row[5] * u)
+            fresh[start + j] = (
                 state.astype(F32) * dcol[:, j : j + 1] + bcol[:, j : j + 1] * u
             ).astype(BF16)
-        h1s[at, :] = rms(blk[...] * H**-0.5, og[...])
+        return rms(jnp.concatenate(reads, axis=0) * H**-0.5, og[...])
 
     order = iota((R1, R1), 0)
     within = order & 15
@@ -323,8 +323,9 @@
     def first_x(k):
         s = lax.rem(k + 1, NX)
         xi = xat(s)
-        each(0, 2, lambda b: first_block(2 * xi + b))
-        h16 = h1s[pl.ds(pl.multiple_of(xi * 16, 16), 16), :].astype(BF16)
+        load_state(2 * xi).wait()
+        load_state(2 * xi + 1).wait()
+        h16 = first_rows(xi * 16, 16).astype(BF16)
         val = dot(dot(perm16, h16).astype(BF16), wo[...])
         for c in range(NCT):
             ax_s1[xi, c] = val[:, cols(c)].astype(BF16)
@@ -335,34 +336,6 @@
 
     each(0, NX, first_x)
     sent.append(lambda: each(1, NX, lambda s: ax_copy(0, s, xx).wait_send()))
-
-    base = dp * R1
-    named[...] = (ids[...] == base + iota((R1, 256), 0)).astype(F32)
-    for s in range(1, ND):
-        pack_copy(s, lax.rem(dp + s, ND)).wait_recv()
-    tp[...] = dot(named[...].astype(BF16), p2all[...].reshape(ND * R2, 4 * H))
-
-    def second_block(i):
-        at = pl.ds(pl.multiple_of(i * 8, 8), 8)
-        t = tp[at, :]
-        for j in range(8):
-            row = [t[j : j + 1, cols(c)] for c in range(4)]
-            a = jnp.where(m == 0, row[0], row[1])
-            got = dot(a.astype(BF16), fresh[i * 8 + j])
-            blk[j : j + 1, :] = got[1:2] + row[3] * (row[2] - got[0:1])
-        h2s[at, :] = rms(blk[...] * H**-0.5, og[...])
-
-    each(0, 8, second_block)
-    h2c[...] = dot(named[...].astype(BF16), h2s[...].astype(BF16), ((0,), (0,))).astype(
-        BF16
-    ).reshape(ND, R2, H)
-
-    def head_copy(s, slot):
-        peer = lax.rem(dp + s, ND)
-        return rcopy(h2c.at[peer], h2r.at[slot], HEAD, s, slot, {"dp": peer})
-
-    each(1, ND, lambda s: head_copy(s, dp).start())
-    sent.append(lambda: each(1, ND, lambda s: head_copy(s, dp).wait_send()))
 
     xp = dot(perm, x1[...])
     x2v = x2[...].astype(F32)
@@ -371,8 +344,6 @@
             rt1[xi, c] = tile(0, xp, xi, c).astype(BF16)
         for c in range(TILES[1]):
             rt2[xi, c] = tile(1, x2v, xi, c).astype(BF16)
-    a_turn(0)
-
     def multi_hot(tab, count):
         hot = jnp.zeros((count, 128), F32)
         for c in range(8):
@@ -404,12 +375,42 @@
         place.append((dot(rank, hot_a.astype(BF16)) == at_a.astype(F32)).astype(F32))
         select.append((dot(hot_b.astype(BF16), rank, ((1,), (1,))) == at_b.astype(F32)).astype(BF16))
 
+    base = dp * R1
+    named[...] = (ids[...] == base + iota((R1, 256), 0)).astype(F32)
+    for s in range(1, ND):
+        pack_copy(s, lax.rem(dp + s, ND)).wait_recv()
+    tp[...] = dot(named[...].astype(BF16), p2all[...].reshape(ND * R2, H))
+
+    def second_rows(k):
+        count = SECOND
+        at = pl.ds(pl.multiple_of(k * count, count), count)
+        t = tp[at, :]
+        reads = []
+        for j in range(count):
+            a = jnp.broadcast_to(t[j : j + 1], (16, H))
+            reads.append(dot(a.astype(BF16), fresh[k * count + j])[0:1])
+        h2s[at, :] = jnp.concatenate(reads, axis=0)
+
+    each(0, R1 // SECOND, second_rows)
+    h2c[...] = dot(named[...].astype(BF16), h2s[...].astype(BF16), ((0,), (0,))).astype(
+        BF16
+    ).reshape(ND, R2, H)
+
+    def head_copy(s, slot):
+        peer = lax.rem(dp + s, ND)
+        return rcopy(h2c.at[peer], h2r.at[slot], HEAD, s, slot, {"dp": peer})
+
+    each(1, ND, lambda s: head_copy(s, dp).start())
+    sent.append(lambda: each(1, ND, lambda s: head_copy(s, dp).wait_send()))
+
+    a_turn(0)
     for s in range(1, ND):
         head_copy(s, lax.rem(dp + s, ND)).wait_recv()
     h2r[dp] = h2c[dp]
     heads2 = h2r[0].astype(F32)
     for g in range(1, ND):
         heads2 = heads2 + h2r[g].astype(F32)
+    heads2 = rms((heads2 + w2[...]) * H**-0.5, og[...])
     a_send(1, dot(heads2.astype(BF16), wo[...]))
     b_start(0)
     a_turn(1)
@@ -618,9 +619,8 @@
     ]
     scratch += [DMA((12,)), DMA((8,)), DMA((SEM_ROWS, 8))]
     scratch += [
-        vm(RT, D), vm(R1, 8 * H, dtype=F32), vm(ND, R2, 4 * H), vm(R1, 256, dtype=F32),
-        vm(R1, 4 * H, dtype=F32), vm(R1, H, H), vm(R1, H, dtype=F32), vm(R1, H, dtype=F32),
-        vm(8, H, dtype=F32), vm(ND, R2, H), vm(ND, R2, H),
+        vm(RT, D), vm(R1, 8 * H, dtype=F32), vm(ND, R2, H), vm(R2, H, dtype=F32), vm(R1, 256, dtype=F32),
+        vm(R1, H, dtype=F32), vm(R1, H, H), vm(R1, H, dtype=F32), vm(ND, R2, H), vm(ND, R2, H),
     ]
     t = (16, 128)
     scratch += both((NX,), t, TILES) + both((NX,), t, TILES)

time: 72.7 us -> 70.7 us (0.972); the launches traced: 72.5 us -> 69.7 us
  Pallas kernels: 71.2 us -> 68.4 us
    pallas_call x1, Pallas kernels: 69.7 us -> 66.9 us  [on_device(): pl.pallas_call(kernel, out_shape=jax.ShapeDtypeStruct((8, D), F32), in_sp...]
where the time goes in v4:
time: 70.7 us; the launch traced here: 69.7 us
  Pallas kernels  68.4 us (97%)
  between operations  1.29 us (2%)
    pallas_call x1, Pallas kernels, on_device(): pl.pallas_call(kernel, out_shape=jax.ShapeDtypeStruct((8, D), F32), in_sp...  66.9 us
    pallas_call x1, Pallas kernels, on_device(): pl.pallas_call(write_kernel, out_shape=(jax.ShapeDtypeStruct((2, D), BF16...  1.5 us

profile of v4, /device:TPU:1, one launch (start us, length us, event | category | flops | bytes accessed | tf_op | source)
XLA Modules:
  0.0 69.7 jit_solution(11037009037760484680)
XLA Ops:
  1.3 66.9 %two_steps.1.final = f32[8,2304]{1,0:T(8,128)} custom-call(bf16[64,2304]{1,0:T(8,128)(2,1)} %x1h.1, bf16[32,2304]{1,0:T(8,128)(2,1)} %x2h.1, bf16[64,128,128]{2,1,0:T(8,128)(2,1)} %bitcast.7, bf16[2304,128]{1,0:T(8,128)(2,1)} %wqh.1, bf16[2304,128]{1,0:T(8,128)(2,1)} %wkh.1, bf16[2304,128]{1,0:T(8,128)(2,1)} %wvh.1, bf16[2304,128]{1,0:T(8,128)(2,1)} %wddh.1, ...), custom_call_target="tpu_custom_call" | custom-call | tf_op jit(solution)/shard_map/two_steps/pallas_call | solution.py:637
  68.2 1.5 %write.1 = (bf16[2,2304]{1,0:T(2,128)(2,1)}, bf16[1,2304]{1,0:T(2,128)(2,1)}) custom-call(f32[8,2304]{1,0:T(8,128)} %two_steps.1.final), custom_call_target="tpu_custom_call" | custom-call | tf_op jit(solution)/shard_map/write/pallas_call | solution.py:653

commit v5 on v4

--- a/solution.py
+++ b/solution.py
@@ -162,13 +162,18 @@
 
     again_row = again[...].reshape(1, D)
     egain_row = egain[...].reshape(1, D)
-    for copy in loads:
+    for copy in loads[0:2]:
+        copy.wait()
+    normed[0:R1, :] = rms(x1[...].astype(F32), again_row).astype(BF16)
+    normed[R1:RT, :] = rms(x2[...].astype(F32), again_row).astype(BF16)
+    n = normed[...]
+    beta = jax.nn.sigmoid(
+        jnp.sum(n.astype(F32) * wb[...].astype(F32), axis=-1, keepdims=True)
+    )
+    for copy in loads[2:]:
         copy.wait()
     for copy in later[1:]:
         copy.start()
-    normed[0:R1, :] = rms(x1[...].astype(F32), again_row).astype(BF16)
-    normed[R1:RT, :] = rms(x2[...].astype(F32), again_row).astype(BF16)
-    n = normed[...]
     every = dot(n, wall[...])
 
     def project(c):
@@ -186,9 +191,6 @@
     soft = jnp.maximum(gate, 0.0) + jnp.log(1.0 + jnp.exp(-jnp.abs(gate)))
     strength = jnp.exp(jnp.full((RT, H), dlog[0], F32))
     decay = jnp.exp(-(strength * soft))
-    beta = jax.nn.sigmoid(
-        jnp.sum(n.astype(F32) * wb[...].astype(F32), axis=-1, keepdims=True)
-    )
     dk = decay * k
     dq = decay * q
     sc = jnp.broadcast_to(beta * jnp.sum(k * q, axis=-1, keepdims=True), (RT, H))

time: 70.7 us -> 70.8 us (level); the launches traced: 69.7 us -> 70.6 us
  Pallas kernels: 68.4 us -> 69.3 us
    pallas_call x1, Pallas kernels: 66.9 us -> 67.8 us  [on_device(): pl.pallas_call(kernel, out_shape=jax.ShapeDtypeStruct((8, D), F32), in_sp...]
where the time goes in v5:
time: 70.8 us; the launch traced here: 70.6 us
  Pallas kernels  69.3 us (98%)
  between operations  1.29 us (2%)
    pallas_call x1, Pallas kernels, on_device(): pl.pallas_call(kernel, out_shape=jax.ShapeDtypeStruct((8, D), F32), in_sp...  67.8 us
    pallas_call x1, Pallas kernels, on_device(): pl.pallas_call(write_kernel, out_shape=(jax.ShapeDtypeStruct((2, D), BF16...  1.5 us

profile of v5, /device:TPU:1, one launch (start us, length us, event | category | flops | bytes accessed | tf_op | source)
XLA Modules:
  0.0 70.6 jit_solution(13347259075917607666)
XLA Ops:
  1.3 67.8 %two_steps.1.final = f32[8,2304]{1,0:T(8,128)} custom-call(bf16[64,2304]{1,0:T(8,128)(2,1)} %x1h.1, bf16[32,2304]{1,0:T(8,128)(2,1)} %x2h.1, bf16[64,128,128]{2,1,0:T(8,128)(2,1)} %bitcast.7, bf16[2304,128]{1,0:T(8,128)(2,1)} %wqh.1, bf16[2304,128]{1,0:T(8,128)(2,1)} %wkh.1, bf16[2304,128]{1,0:T(8,128)(2,1)} %wvh.1, bf16[2304,128]{1,0:T(8,128)(2,1)} %wddh.1, ...), custom_call_target="tpu_custom_call" | custom-call | tf_op jit(solution)/shard_map/two_steps/pallas_call | solution.py:639
  69.0 1.5 %write.1 = (bf16[2,2304]{1,0:T(2,128)(2,1)}, bf16[1,2304]{1,0:T(2,128)(2,1)}) custom-call(f32[8,2304]{1,0:T(8,128)} %two_steps.1.final), custom_call_target="tpu_custom_call" | custom-call | tf_op jit(solution)/shard_map/write/pallas_call | solution.py:655
